TPU v7x, 256 devices: a whole 4x4x8 slice. The times are simulated.
256 devices in a mesh: rows: 128 (over y, z, x), sub: 2 (over core).
Axes of the slice: x: 4, y: 4, z: 8, core: 2. Of those that a mesh axis runs over, the one named last changes fastest.
Arguments:
- embeddings: bfloat16 [262144, 768], P(('rows', 'sub')), may hold values from -0.21875 to 0.21875
- candidates: int32 [2048, 128], P(('rows', 'sub')), may hold values from 0 to 262143, as said below
- fresh_flags: int32 [2048, 128], P(('rows', 'sub')), may hold values 0 or 1
- current: float32 [262144, 32], P(('rows', 'sub')), may hold values from 1.6 to 2.2
Outputs:
- refined: float32 [262144, 32], P(('rows', 'sub'))
Inputs may be any that keep to these rules, and one draw needn't show every extreme that they name: `candidates`: the 8 lists of one device's blocks together name 1024 distinct rows, none owned by that device. Of the 2048 rows of one index of rows, one device's lists name at most 16, and exactly 16 for some such ranges in every device's lists.
All inputs are finite; a program needn't handle non-finite values. No bound on the sum of `fresh_flags` on one device may be relied on, other than what follows from the above.
Results may differ from a plain program's by a relative error of at most 0.0003.
Values may be sent and summed in bfloat16 or wider, within the bound.
A program may use at most 128 MiB of HBM per device.

v0:
```python
import jax
import jax.numpy as jnp
from jax import lax
from jax.sharding import PartitionSpec as P

BLOCK = 128
CAP = 16


FAR_VALUE = 1000000000.0


def partner_2(shard, axis, bit):
    return lax.ppermute(shard, axis, [(i, i ^ 1 << bit) for i in range(lax.axis_size(axis))])


def smallest(values, count):
    return -lax.top_k(-values, count)[0]


def slot_layout(owner_ids, owner_count):
    item_count = owner_ids.shape[0]
    onehot = (owner_ids[:, None] == jnp.arange(owner_count, dtype=jnp.int32)[None, :]).astype(
        jnp.int32
    )
    counts = jnp.sum(onehot, axis=0)
    starts = jnp.cumsum(counts) - counts
    start_of = jnp.sum(onehot * starts[None, :], axis=1)
    order = jnp.argsort(owner_ids, stable=True)
    position = (
        jnp.zeros((item_count,), jnp.int32).at[order].set(jnp.arange(item_count, dtype=jnp.int32))
    )
    rank_slot = position - start_of
    return owner_ids * CAP + rank_slot


def merge_offers(returned, asked_rows, span, neighbours):
    is_live = asked_rows >= 0
    key_rows = jnp.where(is_live, asked_rows, span)
    row_depth = returned.shape[-1]
    row_keys = jnp.broadcast_to(key_rows[..., None], returned.shape).reshape(-1)
    sorted_keys, sorted_vals = lax.sort((row_keys, returned.reshape(-1)), num_keys=2)
    counts = (
        jax.ops.segment_sum(
            is_live.reshape(-1).astype(jnp.int32), key_rows.reshape(-1), num_segments=span + 1
        )[:span]
        * row_depth
    )
    starts = jnp.cumsum(counts) - counts
    offsets = jnp.arange(neighbours, dtype=jnp.int32)
    take_index = jnp.minimum(starts[:, None] + offsets[None, :], sorted_vals.shape[0] - 1)
    return jnp.where(offsets[None, :] < counts[:, None], sorted_vals[take_index], FAR_VALUE)


def per_device(embeddings, candidates, fresh_flags, current):
    rows_dev, row_width = embeddings.shape
    blocks_dev, cand_count = candidates.shape
    neighbours = current.shape[1]
    lane_count = lax.axis_size("rows")
    chip_span = 2 * rows_dev
    flat_ids = candidates.reshape(-1)
    chip_rows = lax.all_gather(embeddings, "sub", axis=0, tiled=True)
    owner_chip = flat_ids // chip_span
    slot_ids = slot_layout(owner_chip, lane_count)
    slot_total = lane_count * CAP
    wanted = jnp.full((slot_total,), -1, jnp.int32).at[slot_ids].set(flat_ids % chip_span)
    asked_rows = lax.all_to_all(
        wanted.reshape(lane_count, CAP), "rows", split_axis=0, concat_axis=0, tiled=True
    )
    safe_rows = jnp.where(asked_rows >= 0, asked_rows, 0).reshape(-1)
    served = jnp.take(chip_rows, safe_rows, axis=0).reshape(lane_count, CAP, row_width)
    pulled = lax.all_to_all(served, "rows", split_axis=0, concat_axis=0, tiled=True)
    cand_rows = jnp.take(pulled.reshape(slot_total, row_width), slot_ids, axis=0)
    cand_rows = cand_rows.reshape(blocks_dev, cand_count, row_width)
    own_rows = embeddings.reshape(blocks_dev, BLOCK, row_width)
    own_norm = jnp.sum(jnp.square(own_rows.astype(jnp.float32)), axis=2)
    cand_norm = jnp.sum(jnp.square(cand_rows.astype(jnp.float32)), axis=2)
    cross_dot = jnp.einsum("bid,bjd->bij", own_rows, cand_rows, preferred_element_type=jnp.float32)
    forward = own_norm[:, :, None] + cand_norm[:, None, :] - 2.0 * cross_dot
    inner_dot = jnp.einsum("bjd,bld->bjl", cand_rows, cand_rows, preferred_element_type=jnp.float32)
    among_dist = cand_norm[:, :, None] + cand_norm[:, None, :] - 2.0 * inner_dot
    fresh_bool = fresh_flags > 0
    diagonal_mask = jnp.eye(cand_count, dtype=jnp.bool_)
    keep_pair = (fresh_bool[:, :, None] | fresh_bool[:, None, :]) & (~diagonal_mask)[None, :, :]
    among_dist = jnp.where(keep_pair, among_dist, FAR_VALUE)
    backward = jnp.concatenate([jnp.swapaxes(forward, 1, 2), among_dist], axis=2)
    backward = backward.reshape(blocks_dev * cand_count, BLOCK + cand_count)
    payload = smallest(backward, neighbours)
    row_depth = payload.shape[1]
    outgoing = jnp.full((slot_total, row_depth), FAR_VALUE, jnp.float32).at[slot_ids].set(payload)
    returned = lax.all_to_all(
        outgoing.reshape(lane_count, CAP, row_depth),
        "rows",
        split_axis=0,
        concat_axis=0,
        tiled=True,
    )
    chip_reverse = merge_offers(returned, asked_rows, chip_span, neighbours)
    my_side = lax.axis_index("sub")
    mine_half = lax.dynamic_slice_in_dim(chip_reverse, my_side * rows_dev, rows_dev, 0)
    other_half = lax.dynamic_slice_in_dim(chip_reverse, (1 - my_side) * rows_dev, rows_dev, 0)
    partner = partner_2(other_half, "sub", 0)
    pool_dist = jnp.concatenate(
        [current, forward.reshape(rows_dev, cand_count), mine_half, partner], axis=1
    )
    return smallest(pool_dist, neighbours)


def solution(mesh):
    in_specs = (
        P(("rows", "sub"), None),
        P(("rows", "sub"), None),
        P(("rows", "sub"), None),
        P(("rows", "sub"), None),
    )
    out_specs = P(("rows", "sub"), None)
    return jax.shard_map(
        per_device, mesh=mesh, in_specs=in_specs, out_specs=out_specs, check_vma=False
    )
```

profile of v0, /device:TPU:1, one launch (start us, length us, event | category | flops | bytes accessed | tf_op | source)
XLA Modules:
  0.0 682.8 jit_solution(14832079531787192529)
XLA Ops:
  7.3 4.4 sort.44
  12.3 4.3 scatter_custom_fusion
  17.0 4.3 scatter_custom_fusion.1
  21.4 26.7 %all_to_all.25 = s32[128,1,16]{2,1,0:T(1,128)S(1)} all-to-all(s32[128,1,16]{2,1,0:T(1,128)S(1)} %bitcast.66), channel_id=1, replica_groups=mesh['rows'=128,'sub'=2] {'rows'}, dimensions={0} | all-to-all | bytes 16384 | tf_op jit(solution)/shard_map/all_to_all | solution.py:67
  49.8 10.8 %gather_fusion = bf16[2048,768]{1,0:T(8,128)(2,1)S(1)} fusion(bf16[2048,768]{1,0:T(8,128)(2,1)} %all-gather.2.cloned.1.call-done, s32[2048]{0:T(1024)S(1)} %broadcast_clamp_fusion.1), kind=kCustom, calls=%fused_computation | custom fusion | bytes 6299648 | tf_op jit(solution)/shard_map/jit(_take)/gather | solution.py:71
  60.6 1.9 broadcast_select_fusion
  62.5 6.2 all-to-all-start.1
  68.8 1.8 multiply_reduce_fusion.1
  70.7 12.4 %scatter_custom_fusion.2 = s32[2049]{0:T(1024)S(1)} fusion(s32[2048]{0:T(1024)S(1)} %bitcast.71, s32[2048]{0:T(1024)S(1)} %reshape.300, s32[]{:T(128)} %constant.104.clone.1), kind=kCustom, calls=%fused_computation.50 | custom fusion | flops 2048 | bytes 8200 | tf_op jit(solution)/shard_map/scatter-add | solution.py:44
  84.3 1.3 compare_select_fusion
  85.7 1.5 reshape.274
  87.2 52.5 %all-to-all-done.1 = bf16[128,16,768]{2,1,0:T(8,128)(2,1)S(1)} async-done(((bf16[128,16,768]{2,1,0:T(8,128)(2,1)}), bf16[128,16,768]{2,1,0:T(8,128)(2,1)S(1)}, u32[]{:S(2)}, u32[]{:S(2)}) %all-to-all-start.1) | async-done | bytes 3145760 | tf_op jit(solution)/shard_map/all_to_all | solution.py:72
  139.6 5.2 gather_fusion.1
  144.9 2.2 multiply_reduce_fusion
  147.1 2.2 fusion.2
  152.2 24.3 %top_k.14 = (f32[1024,256]{0,1:T(8,128)S(1)}, s32[1024,256]{0,1:T(8,128)}) sort(f32[1024,256]{0,1:T(8,128)S(1)} %copy.35, s32[1024,256]{0,1:T(8,128)S(1)} %iota.45.clone), dimensions={1}, to_apply=%region_9.10 | sort | flops 4718592 | bytes 4194304 | tf_op jit(solution)/shard_map/top_k | solution.py:18
  176.9 3.4 scatter_custom_fusion.3
  181.4 10.3 %all-to-all-start.2 = ((f32[128,1,512]{2,1,0:T(1,128)}), f32[128,1,512]{2,1,0:T(1,128)S(1)}, u32[]{:S(2)}, u32[]{:S(2)}) async-start(f32[128,1,512]{2,1,0:T(1,128)} %reshape.341), calls=%async_computation.2 | async-start | bytes 524288 | tf_op jit(solution)/shard_map/all_to_all | solution.py:91
  192.4 11.2 %all-to-all-done.2 = f32[128,1,512]{2,1,0:T(1,128)S(1)} async-done(((f32[128,1,512]{2,1,0:T(1,128)}), f32[128,1,512]{2,1,0:T(1,128)S(1)}, u32[]{:S(2)}, u32[]{:S(2)}) %all-to-all-start.2) | async-done | bytes 262176 | tf_op jit(solution)/shard_map/all_to_all | solution.py:91
  204.2 1.3 reduce.14
  206.1 74.7 %sort.45 = (s32[65536]{0:T(1024)}, f32[65536]{0:T(1024)S(1)}, s32[65536]{0:T(1024)}) sort(s32[65536]{0:T(1024)S(1)} %reshape.251, f32[65536]{0:T(1024)S(1)} %reshape.253, s32[65536]{0:T(1024)S(1)} %iota.46), dimensions={0}, to_apply=%region_11.12 | sort | flops 1048576 | bytes 1572864 | tf_op jit(solution)/shard_map/sort | solution.py:42
  280.8 362.7 %gather_fusion.2 = f32[65536]{0:T(1024)S(1)} fusion(f32[65536]{0:T(1024)S(1)} %get-tuple-element.15, s32[65536]{0:T(1024)S(1)} %broadcast_clamp_fusion), kind=kCustom, calls=%fused_computation.2 | custom fusion | bytes 786432 | tf_op jit(solution)/shard_map/gather | solution.py:52
  644.2 3.8 collective-permute-start
  650.5 24.4 %top_k.20 = (f32[1024,224]{0,1:T(8,128)S(1)}, s32[1024,224]{0,1:T(8,128)}) sort(f32[1024,224]{0,1:T(8,128)S(1)} %copy.39, s32[1024,224]{0,1:T(8,128)S(1)} %iota.47.clone), dimensions={1}, to_apply=%region_14.15 | sort | flops 4128768 | bytes 3670016 | tf_op jit(solution)/shard_map/top_k | solution.py:18
  (72 shorter events, 14.8 us)
Async XLA Ops:
  6.5 0.7 copy-start.5
  6.5 43.3 %all-gather.2.cloned.1.call-start = ((), (), s32[]{:S(2)}) async-start(), calls=%async_computation.3 | async-start | bytes 4718592 | tf_op jit(solution)/shard_map/all_gather | solution.py:62
  62.5 77.1 %all-to-all-start.1 = ((bf16[128,16,768]{2,1,0:T(8,128)(2,1)}), bf16[128,16,768]{2,1,0:T(8,128)(2,1)S(1)}, u32[]{:S(2)}, u32[]{:S(2)}) async-start(bf16[128,16,768]{2,1,0:T(8,128)(2,1)} %broadcast_select_fusion), calls=%async_computation.1 | async-start | bytes 6291456 | tf_op jit(solution)/shard_map/all_to_all | solution.py:72
  68.8 1.8 copy-start.6
  144.9 2.2 copy-start
  147.1 2.4 copy-start.1
  181.4 22.2 %all-to-all-start.2 = ((f32[128,1,512]{2,1,0:T(1,128)}), f32[128,1,512]{2,1,0:T(1,128)S(1)}, u32[]{:S(2)}, u32[]{:S(2)}) async-start(f32[128,1,512]{2,1,0:T(1,128)} %reshape.341), calls=%async_computation.2 | async-start | bytes 524288 | tf_op jit(solution)/shard_map/all_to_all | solution.py:91
  280.8 363.0 %copy-start.4 = (s32[2048]{0:T(1024)S(1)}, s32[2048]{0:T(1024)}, u32[]{:S(2)}) copy-start(s32[2048]{0:T(1024)} %get-tuple-element.27) | copy-start | bytes 24580
  644.1 3.9 copy-start.3
  644.1 4.1 copy-start.2
  644.2 5.3 collective-permute-start
Sparse Core Ops, SparseCore 0:
  9.2 21.9 all-gather.1
where the time goes:
time: 691 us; the launch traced here: 683 us
  local copies, waits for them, and re-layouts  395 us (57%)
  other arithmetic  158 us (23%)
  waiting for transfers between devices  65.6 us (9%)
  blocking collectives  26.7 us (4%)
  starting transfers between devices  20.3 us (3%)
  between operations  14.2 us (2%)
    gather x2, local copies, waits for them, and re-layouts, merge_offers(): sorted_vals[take_index]  363 us
    sort x1, other arithmetic, merge_offers(): lax.sort((row_keys, returned.reshape(-1)), num_keys=2)  74.7 us
    all_to_all x1, waiting for transfers between devices, per_device(): lax.all_to_all(served, 'rows', split_axis=0, concat_axis=0, tiled=True)  52.5 us
    top_k x2, other arithmetic, smallest(): return -lax.top_k(-values, count)[0]  48.6 us
    all_to_all x1, blocking collectives, per_device(): lax.all_to_all(wanted.reshape(lane_count, CAP), 'rows', split_axis=0, con...  26.7 us
  transfers between devices with their start and end apart: 4, of which 3 were waited for; matrix products, arithmetic and copies ran while one was open for 5% of the time, Pallas kernels for 0%

commit v1 on v0

v1 whole, which is shorter than its diff:
```python
import functools

import jax
import jax.numpy as jnp
from jax import lax
from jax.experimental import pallas as pl
from jax.experimental.pallas import tpu as pltpu
from jax.sharding import PartitionSpec as P

BLOCK = 128
CAP = 16
K = 32
FAR = 1.0e9
F32, BF16, I32 = jnp.float32, jnp.bfloat16, jnp.int32
NT = (((1,), (1,)), ((), ()))
NN = (((1,), (0,)), ((), ()))
PITCH = 40


def dot(a, b, dims):
    return lax.dot_general(a, b, dims, preferred_element_type=F32)


def sort_pairs(n):
    pairs = []
    p = 1
    while p < n:
        k = p
        while k >= 1:
            for j in range(k % p, n - k, 2 * k):
                for i in range(min(k, n - j - k)):
                    if (i + j) // (2 * p) == (i + j + k) // (2 * p):
                        pairs.append((i + j, i + j + k))
            k //= 2
        p *= 2
    return pairs


SORT = sort_pairs(K)


def exchange(v, i, j):
    v[i], v[j] = jnp.minimum(v[i], v[j]), jnp.maximum(v[i], v[j])


def sort_list(values):
    v = list(values)
    for i, j in SORT:
        exchange(v, i, j)
    return v


def merge_low(mins):
    v = list(mins)
    d = K // 2
    while d >= 1:
        for i in range(K):
            if i & d == 0:
                exchange(v, i, i + d)
        d //= 2
    return v


def merge_lists(a, b):
    return merge_low([jnp.minimum(a[i], b[K - 1 - i]) for i in range(K)])


def split2(x):
    hi = x.astype(BF16)
    mid = (x - hi.astype(F32)).astype(BF16)
    return hi, mid


def iota(shape, dim):
    return lax.broadcasted_iota(I32, shape, dim)


def onehot(mask):
    return jnp.where(mask, 1.0, 0.0).astype(BF16)


def layout_kernel(span_bits, c_ref, w_ref, s_ref):
    blocks, n = c_ref.shape
    chips = w_ref.shape[0]
    owners = iota((chips, n), 0)
    before = onehot(iota((n, n), 0) < iota((n, n), 1))
    ranks = iota((CAP, n), 0)
    run = jnp.zeros((chips, 1), F32)
    acc = jnp.zeros((chips, 2 * CAP), F32)
    for b in range(blocks):
        c = c_ref[b : b + 1, :]
        owner = lax.shift_right_logical(c, span_bits)
        row1 = (c & ((1 << span_bits) - 1)) + 1
        mine = owner == owners
        mine_b = onehot(mine)
        pre = dot(mine_b, before, NN) + run
        rank = jnp.sum(jnp.where(mine, pre, 0.0), axis=0, keepdims=True).astype(I32)
        run = run + jnp.sum(jnp.where(mine, 1.0, 0.0), axis=1, keepdims=True)
        s_ref[b : b + 1, :] = owner * CAP + rank
        sel = ranks == rank
        hi = jnp.where(sel, lax.shift_right_logical(row1, 4).astype(F32), 0.0).astype(BF16)
        lo = jnp.where(sel, (row1 & 15).astype(F32), 0.0).astype(BF16)
        acc = acc + dot(mine_b, jnp.concatenate([hi, lo], axis=0), NT)
    w_ref[...] = (acc[:, :CAP] * 16.0 + acc[:, CAP:]).astype(I32) - 1


def layout(candidates, chips, span):
    return pl.pallas_call(
        functools.partial(layout_kernel, span.bit_length() - 1),
        out_shape=(
            jax.ShapeDtypeStruct((chips, CAP), I32),
            jax.ShapeDtypeStruct(candidates.shape, I32),
        ),
        name="layout",
    )(candidates)


def serve_kernel(a_ref, rows_ref, out_ref):
    span = rows_ref.shape[0]
    step = out_ref.shape[0]
    asked = a_ref[0].T
    for c in range(step // 128):
        hit = asked[:, c : c + 1] == iota((128, span), 1)
        out_ref[c * 128 : (c + 1) * 128, :] = dot(onehot(hit), rows_ref[...], NN).astype(BF16)


def serve(asked, rows):
    span, width = rows.shape
    slots = asked.size
    per = 8
    steps = slots // (128 * per)
    return pl.pallas_call(
        serve_kernel,
        grid=(steps,),
        in_specs=[
            pl.BlockSpec((1, per, 128), lambda i: (i, 0, 0)),
            pl.BlockSpec((span, width), lambda i: (0, 0)),
        ],
        out_specs=pl.BlockSpec((128 * per, width), lambda i: (i, 0)),
        out_shape=jax.ShapeDtypeStruct((slots, width), BF16),
        compiler_params=pltpu.CompilerParams(vmem_limit_bytes=40 << 20),
        name="serve",
    )(asked.reshape(steps, per, 128), rows)


def plan_kernel(a_ref, pos_ref, row_ref, start_ref, info_ref, key_ref, lv_ref, col_ref, acc_ref, end_ref):
    rows_dev = start_ref.shape[0]
    nrow = a_ref.shape[0]
    slots = nrow * 128
    a = a_ref[...]
    live = (a >= 0) & (a < rows_dev)
    sid = iota((nrow, 128), 0) * 128 + iota((nrow, 128), 1)
    key = jnp.where(live, a * slots + sid, (1 << 30) + sid)
    key_ref[...] = key
    lv_ref[...] = jnp.where(live, a, rows_dev)
    for h in range(nrow // 8):
        col_ref[:, h * 8 : (h + 1) * 8] = key[h * 8 : (h + 1) * 8, :].T
    acc_ref[...] = jnp.zeros_like(acc_ref)
    lane = iota((128, nrow), 1)

    def outer(c, carry):
        col = jnp.sum(jnp.where(lane == c, col_ref[...], 0), axis=1, keepdims=True)
        colb = jnp.broadcast_to(col, (128, 128))

        def inner(e, carry):
            less = jnp.where(colb < key_ref[pl.ds(e, 1), :], 1.0, 0.0)
            part = jnp.sum(less.reshape(16, 8, 128), axis=0)
            at = pl.ds(pl.multiple_of(e * 8, 8), 8)
            acc_ref[at, :] = acc_ref[at, :] + part
            return carry

        return lax.fori_loop(0, nrow, inner, carry)

    lax.fori_loop(0, nrow, outer, 0)
    for e in range(nrow):
        pos_ref[e : e + 1, :] = jnp.sum(acc_ref[e * 8 : (e + 1) * 8, :], axis=0, keepdims=True).astype(I32)

    def start_of(g, most):
        v = g * 128 + iota((128, 128), 0)
        low = jnp.zeros((128, 128), F32)
        own = jnp.zeros((128, 128), F32)
        for e in range(nrow):
            lv = lv_ref[e : e + 1, :]
            low = low + jnp.where(lv < v, 1.0, 0.0)
            own = own + jnp.where(lv == v, 1.0, 0.0)
        start = jnp.sum(low, axis=1, keepdims=True)
        count = jnp.sum(own, axis=1, keepdims=True)
        at = pl.ds(pl.multiple_of(g * 128, 128), 128)
        end_ref[at, :] = jnp.broadcast_to((start + count).astype(I32), (128, 128))
        start_ref[at, :] = jnp.broadcast_to(jnp.where(count > 0, start, -1.0).astype(I32), (128, 128))
        return jnp.maximum(most, jnp.max(count))

    most = lax.fori_loop(0, rows_dev // 128, start_of, jnp.float32(0))
    total = jnp.sum(jnp.where(live, 1.0, 0.0)).astype(I32)
    info_ref[0] = total
    info_ref[1] = most.astype(I32)
    row_ref[...] = jnp.full(row_ref.shape, rows_dev, I32)

    def row_of(c, carry):
        p = c * 128 + iota((8, 128), 1)
        acc = jnp.zeros((8, 128), F32)
        for g in range(rows_dev // 8):
            acc = acc + jnp.where(end_ref[g * 8 : (g + 1) * 8, :] <= p, 1.0, 0.0)
        row = jnp.sum(acc, axis=0, keepdims=True).astype(I32)
        row_ref[pl.ds(c, 1), :] = jnp.where(p[0:1, :] < total, row, rows_dev)
        return carry

    lax.fori_loop(0, nrow, row_of, 0)


def plan(asked_rows, rows_dev):
    nrow = asked_rows.shape[0]
    return pl.pallas_call(
        plan_kernel,
        out_shape=(
            jax.ShapeDtypeStruct((nrow, 128), I32),
            jax.ShapeDtypeStruct((PITCH, 128), I32),
            jax.ShapeDtypeStruct((rows_dev, 128), I32),
            jax.ShapeDtypeStruct((2,), I32),
        ),
        out_specs=(
            pl.BlockSpec(memory_space=pltpu.VMEM),
            pl.BlockSpec(memory_space=pltpu.VMEM),
            pl.BlockSpec(memory_space=pltpu.VMEM),
            pl.BlockSpec(memory_space=pltpu.SMEM),
        ),
        scratch_shapes=[
            pltpu.VMEM((nrow, 128), I32),
            pltpu.VMEM((nrow, 128), I32),
            pltpu.VMEM((128, nrow), I32),
            pltpu.VMEM((nrow * 8, 128), F32),
            pltpu.VMEM((rows_dev, 128), I32),
        ],
        cost_estimate=pl.CostEstimate(flops=20_000_000_000, bytes_accessed=1_000_000, transcendentals=0),
        name="plan",
    )(asked_rows)


def join_kernel(pulled_ref, own_ref, slot_ref, flag_ref, out_ref, fwd_ref, z_ref, f_ref, a_ref, t_ref, hot_ref, pay_ref):
    blocks = slot_ref.shape[0]
    slots = pulled_ref.shape[0]
    slot_cols = slot_ref[...].T
    flags = flag_ref[...]
    flag_cols = flags.T
    ids = iota((128, slots), 1)
    r2, c2 = iota((256, 256), 0), iota((256, 256), 1)
    eye = r2 == c2
    off_diag = iota((128, 128), 0) != iota((128, 128), 1)
    for b in range(blocks):
        at = slice(b * 128, (b + 1) * 128)
        pick = onehot(slot_cols[:, b : b + 1] == ids)
        z_ref[0:128, :] = own_ref[at, :]
        z_ref[128:256, :] = dot(pick, pulled_ref[...], NN).astype(BF16)
        z = z_ref[...]
        gram = dot(z, z, NT)
        diag = jnp.where(eye, gram, 0.0)
        n_col = jnp.sum(diag, axis=1, keepdims=True)
        n_row = jnp.sum(diag, axis=0, keepdims=True)
        dist = n_col + n_row - 2.0 * gram
        f_ref[at, :] = dist[0:128, 128:256]
        fwd_ref[at, :] = dist[128:256, 0:128]
        fresh = (flag_cols[:, b : b + 1] + flags[b : b + 1, :]) > 0
        a_ref[at, :] = jnp.where(fresh & off_diag, dist[128:256, 128:256], FAR)

    def take(ref, g):
        return [ref[pl.ds(g * K + t, 8, stride=128), :] for t in range(K)]

    best = sort_list(take(f_ref, 0))

    def more(ref, lo, best):
        def body(g, best):
            return tuple(merge_lists(list(best), sort_list(take(ref, g))))

        return lax.fori_loop(lo, 128 // K, body, tuple(best))

    best = more(f_ref, 1, best)
    best = more(a_ref, 0, best)
    for k in range(K):
        t_ref[k * 8 : (k + 1) * 8, :] = best[k]
    quad = lax.shift_right_logical(iota((128, 128), 0), 5)
    groups = iota((slots // 4, 128), 0)
    for b in range(blocks):
        at = slice(b * 128, (b + 1) * 128)
        slot = slot_ref[b : b + 1, :]
        mine = t_ref[pl.ds(b, K, stride=8), :]
        tiled = jnp.concatenate([mine] * 4, axis=0)
        hi, mid = split2(jnp.where((slot & 3) == quad, tiled, 0.0))
        pay_ref[0:128, at] = hi
        pay_ref[128:256, at] = mid
        hot_ref[:, at] = onehot(lax.shift_right_logical(slot, 2) == groups)
    both = dot(hot_ref[...], pay_ref[...], NT)
    out_ref[...] = both[:, 0:128] + both[:, 128:256]


def join(pulled, own, slots, flags):
    n = pulled.shape[0]
    rows, width = own.shape
    return pl.pallas_call(
        join_kernel,
        out_shape=(
            jax.ShapeDtypeStruct((n // 4, 128), F32),
            jax.ShapeDtypeStruct((rows, 128), F32),
        ),
        scratch_shapes=[
            pltpu.VMEM((256, width), BF16),
            pltpu.VMEM((rows, 128), F32),
            pltpu.VMEM((rows, 128), F32),
            pltpu.VMEM((K * 8, 128), F32),
            pltpu.VMEM((n // 4, rows), BF16),
            pltpu.VMEM((256, rows), BF16),
        ],
        compiler_params=pltpu.CompilerParams(vmem_limit_bytes=40 << 20),
        name="join",
    )(pulled, own, slots, flags)


def near_kernel(fwd_ref, cur_ref, out_ref, s_ref):
    blocks = cur_ref.shape[0] // 128
    for b in range(blocks):
        s_ref[b * K : (b + 1) * K, :] = cur_ref[b * 128 : (b + 1) * 128, :].T
    best = sort_list([s_ref[pl.ds(k, 8, stride=K), :] for k in range(K)])

    def body(g, best):
        more = [fwd_ref[pl.ds(g * K + t, 8, stride=128), :] for t in range(K)]
        return tuple(merge_lists(list(best), sort_list(more)))

    best = lax.fori_loop(0, 128 // K, body, tuple(best))
    for k in range(K):
        out_ref[k * 8 : (k + 1) * 8, :] = best[k]


def near(fwd, current):
    return pl.pallas_call(
        near_kernel,
        out_shape=jax.ShapeDtypeStruct((K * 8, 128), F32),
        scratch_shapes=[pltpu.VMEM((current.shape[0] // 128 * K, 128), F32)],
        cost_estimate=pl.CostEstimate(flops=8_000_000_000, bytes_accessed=1_000_000, transcendentals=0),
        name="near",
    )(fwd, current)


def merge_kernel(mine_ref, his_ref, pos_ref, row_ref, start_ref, info_ref, near_ref, out_ref, pay_ref, s_ref, x_ref, acc_ref):
    half = mine_ref.shape[0]
    rows_dev = out_ref.shape[0]
    lanes = iota((half, 128), 1)
    total = info_ref[0]
    most = info_ref[1]
    for h, ref in enumerate((mine_ref, his_ref)):
        vals = ref[...]
        for q in range(4):
            at = slice((q * 2 + h) * half, (q * 2 + h + 1) * half)
            hi, mid = split2(jnp.where(lax.shift_right_logical(lanes, 5) == q, vals, 0.0))
            pay_ref[at, 0:128] = hi
            pay_ref[at, 128:256] = mid
    s_ref[...] = jnp.full(s_ref.shape, FAR, F32)
    chunks = (total + 127) // 128
    width = pay_ref.shape[0]

    def gather(c, carry):
        p = c * 128 + iota((128, width), 0)
        got = dot(onehot(pos_ref[...] == p), pay_ref[...], NN)
        turned = (got[:, 0:128] + got[:, 128:256]).T
        vals = turned[0:32] + turned[32:64] + turned[64:96] + turned[96:128]
        s_ref[pl.ds(c, K, stride=PITCH), :] = vals
        return carry

    lax.fori_loop(0, chunks, gather, 0)
    lane = iota((8, 128), 1)
    groups = (total + 1023) // 1024

    def ahead(ref, at, s):
        here = ref[pl.ds(at, 8), :]
        after = ref[pl.ds(at + 1, 8), :]
        return after if s == 128 else pltpu.roll(jnp.where(lane >= s, here, after), 128 - s, 1)

    for e in range(8):

        @pl.when(most > 1 << e)
        def _():
            def step(g, carry):
                at = pl.multiple_of(g * 8, 8)
                same = row_ref[pl.ds(at, 8), :] == ahead(row_ref, at, 1 << e)
                mins = []
                for k in range(K):
                    later = ahead(s_ref, (K - 1 - k) * PITCH + at, 1 << e)
                    mins.append(jnp.minimum(s_ref[pl.ds(k * PITCH + at, 8), :], jnp.where(same, later, FAR)))
                best = merge_low(mins)
                for k in range(K):
                    s_ref[pl.ds(k * PITCH + at, 8), :] = best[k]
                return carry

            lax.fori_loop(0, groups, step, 0)

    acc_ref[...] = jnp.zeros_like(acc_ref)

    def expand(c, carry):
        vals = s_ref[pl.ds(c, K, stride=PITCH), :]
        live = c * 128 + iota((K, 128), 1) < total
        hi, mid = split2(jnp.where(live, vals, 0.0))
        p = c * 128 + iota((rows_dev, 128), 1)
        hot = onehot(start_ref[...] == p)
        ones = jnp.ones((K // 2, 128), BF16)
        acc_ref[...] = acc_ref[...] + dot(jnp.concatenate([hi, mid, ones], axis=0), hot, NT)
        return carry

    lax.fori_loop(0, chunks, expand, 0)
    for b in range(rows_dev // 128):
        at = slice(b * 128, (b + 1) * 128)
        named = acc_ref[2 * K : 2 * K + 1, at] > 0.5
        x_ref[b * K : (b + 1) * K, :] = jnp.where(named, acc_ref[0:K, at] + acc_ref[K : 2 * K, at], FAR)
    have = near_ref[...]
    got = [x_ref[pl.ds(k, 8, stride=K), :] for k in range(K)]
    mins = [
        jnp.minimum(have[k * 8 : (k + 1) * 8, :], got[K - 1 - k])
        for k in range(K)
    ]
    best = merge_low(mins)
    for k in range(K):
        x_ref[k * 8 : (k + 1) * 8, :] = best[k]
    for b in range(rows_dev // 128):
        out_ref[b * 128 : (b + 1) * 128, :] = x_ref[pl.ds(b, K, stride=8), :].T


def merge(mine, his, pos, row, start, info, best):
    rows_dev = start.shape[0]
    vmem = pl.BlockSpec(memory_space=pltpu.VMEM)
    return pl.pallas_call(
        merge_kernel,
        in_specs=[vmem] * 5 + [pl.BlockSpec(memory_space=pltpu.SMEM), vmem],
        out_specs=vmem,
        out_shape=jax.ShapeDtypeStruct((rows_dev, K), F32),
        scratch_shapes=[
            pltpu.VMEM((pos.shape[1], 256), BF16),
            pltpu.VMEM((K * PITCH, 128), F32),
            pltpu.VMEM((rows_dev // 128 * K, 128), F32),
            pltpu.VMEM((2 * K + K // 2, rows_dev), F32),
        ],
        compiler_params=pltpu.CompilerParams(vmem_limit_bytes=40 << 20),
        name="merge",
    )(mine, his, pos, row, start, info, best)


def per_device(embeddings, candidates, fresh_flags, current):
    rows_dev = embeddings.shape[0]
    chips = lax.axis_size("rows")
    sides = lax.axis_size("sub")
    swap = [(i, i ^ 1) for i in range(sides)]
    span = sides * rows_dev
    total = chips * CAP
    wanted, slots = layout(candidates, chips, span)
    chip_rows = lax.all_gather(embeddings, "sub", axis=0, tiled=True)
    asked = lax.all_to_all(wanted, "rows", split_axis=0, concat_axis=0, tiled=True)
    served = serve(asked.reshape(total // 128, 128), chip_rows)
    pulled = lax.all_to_all(
        served.reshape(chips, CAP, -1), "rows", split_axis=0, concat_axis=0, tiled=True
    ).reshape(total, -1)
    his_asked = lax.ppermute(asked, "sub", swap)
    here = jnp.stack([asked, his_asked]) - lax.axis_index("sub") * rows_dev
    here = here.reshape(2, chips, CAP // 4, 4).transpose(3, 0, 1, 2).reshape(-1, 128)
    pos, row, start, info = plan(here, rows_dev)
    outgoing, fwd = join(pulled, embeddings, slots, fresh_flags)
    returned = lax.all_to_all(
        outgoing.reshape(chips, CAP // 4, 128), "rows", split_axis=0, concat_axis=0, tiled=True
    ).reshape(total // 4, 128)
    best = near(fwd, current)
    his = lax.ppermute(returned, "sub", swap)
    return merge(returned, his, pos.reshape(1, -1), row, start, info, best)


def solution(mesh):
    spec = P(("rows", "sub"), None)
    return jax.shard_map(
        per_device, mesh=mesh, in_specs=(spec,) * 4, out_specs=spec, check_vma=False
    )
```

time: 691 us -> 204 us (0.30); the launches traced: 683 us -> 203 us
  local copies, waits for them, and re-layouts: 395 us -> 12 us
  other arithmetic: 158 us -> 0.81 us
  Pallas kernels: 0 us -> 62.4 us
    gather x4 -> x0, local copies, waits for them, and re-layouts: 379 us -> none  [the longest x2 363 us: merge_offers(): sorted_vals[take_index]]
    sort x2 -> x0, other arithmetic: 79 us -> none  [the longest x1 74.7 us: merge_offers(): lax.sort((row_keys, returned.reshape(-1)), num_keys=2)]
    pallas_call x0 -> x6, Pallas kernels: none -> 62.4 us  [the longest x1 34.1 us: plan(): pl.pallas_call(plan_kernel, out_shape=(jax.ShapeDtypeStruct((nrow, 128),...]
    top_k x2 -> x0, other arithmetic: 48.6 us -> none  [smallest(): return -lax.top_k(-values, count)[0]]
    scatter-add x1 -> x0, other arithmetic: 12.4 us -> none  [merge_offers(): jax.ops.segment_sum(is_live.reshape(-1).astype(jnp.int32), key_rows.resha...]
    scatter x2 -> x0, local copies, waits for them, and re-layouts: 8.63 us -> none  [the longest x1 4.32 us: per_device(): jnp.full((slot_total,), -1, jnp.int32).at[slot_ids]]
  transfers between devices with their start and end apart: 4 -> 5, of which waited for: 3 -> 1; matrix products, arithmetic and copies ran while one was open for 5% -> 3% of each run, Pallas kernels for 0% -> 19%
where the time goes in v1:
time: 204 us; the launch traced here: 203 us
  waiting for transfers between devices  66.8 us (33%)
  Pallas kernels  62.4 us (31%)
  blocking collectives  26.8 us (13%)
  starting transfers between devices  20.5 us (10%)
  between operations  13.5 us (7%)
  local copies, waits for them, and re-layouts  12 us (6%)
    all_to_all x1, waiting for transfers between devices, per_device(): lax.all_to_all(served.reshape(chips, CAP, -1), 'rows', split_axis=0, conc...  66.1 us
    pallas_call x1, Pallas kernels, plan(): pl.pallas_call(plan_kernel, out_shape=(jax.ShapeDtypeStruct((nrow, 128),...  34.1 us
    all_to_all x1, blocking collectives, per_device(): lax.all_to_all(wanted, 'rows', split_axis=0, concat_axis=0, tiled=True)  26.8 us
    all_to_all x1, starting transfers between devices, per_device(): lax.all_to_all(outgoing.reshape(chips, CAP // 4, 128), 'rows', split_axis...  10.1 us
    pallas_call x1, Pallas kernels, join(): pl.pallas_call(join_kernel, out_shape=(jax.ShapeDtypeStruct((n // 4, 128)...  8.9 us
    pallas_call x1, Pallas kernels, merge(): pl.pallas_call(merge_kernel, in_specs=[vmem] * 5 + [pl.BlockSpec(memory_s...  7.68 us
    unnamed x25, local copies, waits for them, and re-layouts  7.64 us
    all_to_all x1, starting transfers between devices, per_device(): lax.all_to_all(served.reshape(chips, CAP, -1), 'rows', split_axis=0, conc...  7.52 us
  transfers between devices with their start and end apart: 5, of which 1 were waited for; matrix products, arithmetic and copies ran while one was open for 3% of the time, Pallas kernels for 19%

profile of v1, /device:TPU:1, one launch (start us, length us, event | category | flops | bytes accessed | tf_op | source)
XLA Modules:
  0.0 203.0 jit_solution(6515951791787271048)
XLA Ops:
  6.5 0.7 all-gather.2.cloned.1.call-update
  7.3 1.8 layout.1
  9.1 26.8 %all_to_all.22 = s32[128,1,16]{2,1,0:T(1,128)S(1)} all-to-all(s32[128,1,16]{2,1,0:T(1,128)} %bitcast.20), channel_id=1, replica_groups=mesh['rows'=128,'sub'=2] {'rows'}, dimensions={0} | all-to-all | bytes 16384 | tf_op jit(solution)/shard_map/all_to_all | solution.py:452
  35.9 0.5 broadcast.4
  36.4 0.8 reduce.3
  37.4 1.9 copy-done.2
  39.2 7.1 %serve.1 = bf16[2048,768]{1,0:T(8,128)(2,1)S(1)} custom-call(s32[2,8,128]{2,1,0:T(8,128)S(1)} %reshape_reshape.3.a_ref, bf16[2048,768]{1,0:T(8,128)(2,1)S(1)} %copy-done.2), custom_call_target="tpu_custom_call" | custom-call | tf_op jit(solution)/shard_map/serve/pallas_call | solution.py:132
  46.4 1.6 copy-done
  48.0 7.5 %all-to-all-start.1 = ((bf16[128,16,768]{2,1,0:T(8,128)(2,1)}), bf16[128,16,768]{2,1,0:T(8,128)(2,1)S(1)}, u32[]{:S(2)}, u32[]{:S(2)}) async-start(bf16[128,16,768]{2,1,0:T(8,128)(2,1)} %bitcast.16), calls=%async_computation.1 | async-start | bytes 6291456 | tf_op jit(solution)/shard_map/all_to_all | solution.py:454
  55.6 1.2 collective-permute-start.1
  56.8 1.0 copy.18.cur_ref
  57.8 1.0 copy.17
  58.8 1.9 reshape.31.a_ref
  60.7 66.1 %all-to-all-done.1 = bf16[128,16,768]{2,1,0:T(8,128)(2,1)S(1)} async-done(((bf16[128,16,768]{2,1,0:T(8,128)(2,1)}), bf16[128,16,768]{2,1,0:T(8,128)(2,1)S(1)}, u32[]{:S(2)}, u32[]{:S(2)}) %all-to-all-start.1) | async-done | bytes 3145760 | tf_op jit(solution)/shard_map/all_to_all | solution.py:454
  126.9 1.4 copy-done.1
  128.3 8.9 %join.1 = (f32[512,128]{1,0:T(8,128)}, f32[1024,128]{1,0:T(8,128)S(1)}) custom-call(bf16[2048,768]{1,0:T(8,128)(2,1)S(1)} %bitcast.15, bf16[1024,768]{1,0:T(8,128)(2,1)S(1)} %copy-done.1, s32[8,128]{1,0:T(8,128)S(1)} %copy-done.8, s32[8,128]{1,0:T(8,128)S(1)} %copy-done.7), custom_call_target="tpu_custom_call" | custom-call | tf_op jit(solution)/shard_map/join/pallas_call | solution.py:298
  137.2 0.8 copy-done.10
  138.0 10.1 %all-to-all-start.2 = ((f32[128,4,128]{2,1,0:T(4,128)}), f32[128,4,128]{2,1,0:T(4,128)S(1)}, u32[]{:S(2)}, u32[]{:S(2)}) async-start(f32[128,4,128]{2,1,0:T(4,128)} %bitcast.4), calls=%async_computation.2 | async-start | bytes 524288 | tf_op jit(solution)/shard_map/all_to_all | solution.py:462
  148.1 34.1 %plan.1 = (s32[32,128]{1,0:T(8,128)}, s32[40,128]{1,0:T(8,128)}, s32[1024,128]{1,0:T(8,128)}, s32[2]{0:T(128)}) custom-call(s32[32,128]{1,0:T(8,128)} %reshape.31.a_ref), custom_call_target="tpu_custom_call" | custom-call | flops 20000000000 | bytes 1000000 | tf_op jit(solution)/shard_map/plan/pallas_call | solution.py:213
  182.2 1.7 collective-permute-start
  184.0 2.7 %near.1.near_ref = f32[256,128]{1,0:T(8,128)} custom-call(f32[1024,128]{1,0:T(8,128)} %copy-done.10, f32[1024,32]{1,0:T(8,128)} %copy.18.cur_ref), custom_call_target="tpu_custom_call" | custom-call | flops 8000000000 | bytes 1000000 | tf_op jit(solution)/shard_map/near/pallas_call | solution.py:333
  186.7 0.9 copy-done.4
  187.6 7.7 %merge.1 = f32[1024,32]{1,0:T(8,128)S(1)} custom-call(f32[512,128]{1,0:T(8,128)S(1)} %bitcast.18, f32[512,128]{1,0:T(8,128)S(1)} %collective-permute-done.his_ref, s32[1,4096]{1,0:T(1,128)S(1)} %bitcast.19, s32[40,128]{1,0:T(8,128)S(1)} %copy-done.5, s32[1024,128]{1,0:T(8,128)S(1)} %copy-done.3, s32[2]{0:T(128)S(1)} %copy-done.9, f32[256,128]{1,0:T(8,128)S(1)} %copy-done.4), custom_call_target="tpu_custom_call" | custom-call | tf_op jit(solution)/shard_map/merge/pallas_call | solution.py:427
  195.3 0.8 copy.19
  (27 shorter events, 0.2 us)
Async XLA Ops:
  6.5 30.8 %all-gather.2.cloned.1.call-start = ((), (), s32[]{:S(2)}) async-start(), calls=%async_computation.3 | async-start | bytes 4718592 | tf_op jit(solution)/shard_map/all_gather | solution.py:451
  37.3 1.9 copy-start.2
  46.4 1.7 copy-start
  48.0 8.8 %copy-start.11 = (f32[1024,32]{0,1:T(8,128)S(1)}, f32[1024,32]{0,1:T(8,128)}, u32[]{:S(2)}) copy-start(f32[1024,32]{0,1:T(8,128)} %param.7) | copy-start | bytes 393220
  48.0 78.8 %copy-start.7 = (s32[8,128]{1,0:T(8,128)S(1)}, s32[8,128]{1,0:T(8,128)}, u32[]{:S(2)}) copy-start(s32[8,128]{1,0:T(8,128)} %flag_ref.1) | copy-start | bytes 12292
  48.0 78.8 %copy-start.8 = (s32[8,128]{1,0:T(8,128)S(1)}, s32[8,128]{1,0:T(8,128)}, u32[]{:S(2)}) copy-start(s32[8,128]{1,0:T(8,128)} %get-tuple-element.14.slot_ref) | copy-start | bytes 12292
  48.0 78.8 %all-to-all-start.1 = ((bf16[128,16,768]{2,1,0:T(8,128)(2,1)}), bf16[128,16,768]{2,1,0:T(8,128)(2,1)S(1)}, u32[]{:S(2)}, u32[]{:S(2)}) async-start(bf16[128,16,768]{2,1,0:T(8,128)(2,1)} %bitcast.16), calls=%async_computation.1 | async-start | bytes 6291456 | tf_op jit(solution)/shard_map/all_to_all | solution.py:454
  55.6 2.2 %collective-permute-start.1 = (s32[128,16]{0,1:T(8,128)S(1)}, s32[128,16]{0,1:T(8,128)S(1)}, u32[]{:S(2)}, u32[]{:S(2)}) collective-permute-start(s32[128,16]{0,1:T(8,128)S(1)} %bitcast.21), channel_id=1, source_target_pairs={{0,1},{1,0},{2,3},{3,2},{4,5},{5,4},{6,7},{7,6},{8,9},{9,8},{10,11... | collective-permute-start | bytes 24584 | tf_op jit(solution)/shard_map/ppermute | solution.py:457
  126.9 1.4 copy-start.1
  137.2 0.8 copy-start.10
  138.0 44.3 %all-to-all-start.2 = ((f32[128,4,128]{2,1,0:T(4,128)}), f32[128,4,128]{2,1,0:T(4,128)S(1)}, u32[]{:S(2)}, u32[]{:S(2)}) async-start(f32[128,4,128]{2,1,0:T(4,128)} %bitcast.4), calls=%async_computation.2 | async-start | bytes 524288 | tf_op jit(solution)/shard_map/all_to_all | solution.py:462
  182.2 4.4 %collective-permute-start = (f32[512,128]{1,0:T(8,128)S(1)}, f32[512,128]{1,0:T(8,128)S(1)}, u32[]{:S(2)}, u32[]{:S(2)}) collective-permute-start(f32[512,128]{1,0:T(8,128)S(1)} %bitcast.17), channel_id=1, source_target_pairs={{0,1},{1,0},{2,3},{3,2},{4,5},{5,4},{6,7},{7,6},{8,9},{9,8},{10,11... | collective-permute-start | bytes 786440 | tf_op jit(solution)/shard_map/ppermute | solution.py:466
  184.0 2.7 %copy-start.3 = (s32[1024,128]{1,0:T(8,128)S(1)}, s32[1024,128]{1,0:T(8,128)}, u32[]{:S(2)}) copy-start(s32[1024,128]{1,0:T(8,128)} %get-tuple-element.18.start_ref) | copy-start | bytes 1572868
  184.0 2.7 %copy-start.5 = (s32[40,128]{1,0:T(8,128)S(1)}, s32[40,128]{1,0:T(8,128)}, u32[]{:S(2)}) copy-start(s32[40,128]{1,0:T(8,128)} %get-tuple-element.17.row_ref) | copy-start | bytes 61444
  184.0 2.7 %copy-start.6 = (s32[32,128]{1,0:T(8,128)S(1)}, s32[32,128]{1,0:T(8,128)}, u32[]{:S(2)}) copy-start(s32[32,128]{1,0:T(8,128)} %get-tuple-element.16) | copy-start | bytes 49156
  184.0 2.7 %copy-start.9 = (s32[2]{0:T(128)S(1)}, s32[2]{0:T(128)}, u32[]{:S(2)}) copy-start(s32[2]{0:T(128)} %get-tuple-element.19.info_ref) | copy-start | bytes 28
  186.7 0.9 copy-start.4
Sparse Core Ops, SparseCore 0:
  9.2 21.9 all-gather.1

commit v2 on v1

--- a/solution.py
+++ b/solution.py
@@ -15,6 +15,10 @@
 NT = (((1,), (1,)), ((), ()))
 NN = (((1,), (0,)), ((), ()))
 PITCH = 40
+NY, NZ, NX = 4, 8, 4
+PLANE = NY * NX
+FAR_FIRST = (4, 3, 5, 2, 6, 1, 7, 0)
+MESH = pl.DeviceIdType.MESH
 
 
 def dot(a, b, dims):
@@ -79,7 +83,54 @@
     return jnp.where(mask, 1.0, 0.0).astype(BF16)
 
 
-def layout_kernel(span_bits, c_ref, w_ref, s_ref):
+def place():
+    chip = lax.axis_index("rows")
+    return lax.div(chip, NZ * NX), lax.rem(lax.div(chip, NX), NZ), lax.rem(chip, NX), lax.axis_index("sub")
+
+
+def chip_at(y, z, x):
+    return (lax.rem(y, NY) * NZ + lax.rem(z, NZ)) * NX + lax.rem(x, NX)
+
+
+def column_peers(here):
+    y, z, x, side = here
+    return [(dz, {"rows": chip_at(y, z + dz, x), "sub": side}) for dz in FAR_FIRST[:-1]]
+
+
+def plane_peers(here):
+    y, z, x, side = here
+    return [
+        (dy, dx, h, {"rows": chip_at(y + dy, z, x + dx), "sub": lax.rem(side + h, 2)})
+        for dy in range(NY)
+        for dx in range(NX)
+        for h in range(2)
+        if dy + dx + h > 0
+    ]
+
+
+def greet(here):
+    sem = pltpu.get_barrier_semaphore()
+    peers = [p[-1] for p in column_peers(here)] + [p[-1] for p in plane_peers(here)]
+    for device in peers:
+        pl.semaphore_signal(sem, inc=1, device_id=device, device_id_type=MESH)
+    return lambda: pl.semaphore_wait(sem, len(peers))
+
+
+def remote(src, dst, send, recv, device):
+    return pltpu.make_async_remote_copy(
+        src_ref=src, dst_ref=dst, send_sem=send, recv_sem=recv, device_id=device, device_id_type=MESH
+    )
+
+
+def far_rank(dz):
+    return FAR_FIRST.index(dz % NZ)
+
+
+def plane_rank(dy, dx):
+    return (dy % NY) * NX + dx % NX
+
+
+def slots_of(c_ref, w_ref, s_ref, span_bits):
     blocks, n = c_ref.shape
     chips = w_ref.shape[0]
     owners = iota((chips, n), 0)
@@ -89,7 +140,8 @@
     acc = jnp.zeros((chips, 2 * CAP), F32)
     for b in range(blocks):
         c = c_ref[b : b + 1, :]
-        owner = lax.shift_right_logical(c, span_bits)
+        chip = lax.shift_right_logical(c, span_bits)
+        owner = (chip & 28) * 4 + lax.shift_right_logical(chip, 5) * 4 + (chip & 3)
         row1 = (c & ((1 << span_bits) - 1)) + 1
         mine = owner == owners
         mine_b = onehot(mine)
@@ -101,53 +153,14 @@
         hi = jnp.where(sel, lax.shift_right_logical(row1, 4).astype(F32), 0.0).astype(BF16)
         lo = jnp.where(sel, (row1 & 15).astype(F32), 0.0).astype(BF16)
         acc = acc + dot(mine_b, jnp.concatenate([hi, lo], axis=0), NT)
-    w_ref[...] = (acc[:, :CAP] * 16.0 + acc[:, CAP:]).astype(I32) - 1
-
-
-def layout(candidates, chips, span):
-    return pl.pallas_call(
-        functools.partial(layout_kernel, span.bit_length() - 1),
-        out_shape=(
-            jax.ShapeDtypeStruct((chips, CAP), I32),
-            jax.ShapeDtypeStruct(candidates.shape, I32),
-        ),
-        name="layout",
-    )(candidates)
-
-
-def serve_kernel(a_ref, rows_ref, out_ref):
-    span = rows_ref.shape[0]
-    step = out_ref.shape[0]
-    asked = a_ref[0].T
-    for c in range(step // 128):
-        hit = asked[:, c : c + 1] == iota((128, span), 1)
-        out_ref[c * 128 : (c + 1) * 128, :] = dot(onehot(hit), rows_ref[...], NN).astype(BF16)
-
-
-def serve(asked, rows):
-    span, width = rows.shape
-    slots = asked.size
-    per = 8
-    steps = slots // (128 * per)
-    return pl.pallas_call(
-        serve_kernel,
-        grid=(steps,),
-        in_specs=[
-            pl.BlockSpec((1, per, 128), lambda i: (i, 0, 0)),
-            pl.BlockSpec((span, width), lambda i: (0, 0)),
-        ],
-        out_specs=pl.BlockSpec((128 * per, width), lambda i: (i, 0)),
-        out_shape=jax.ShapeDtypeStruct((slots, width), BF16),
-        compiler_params=pltpu.CompilerParams(vmem_limit_bytes=40 << 20),
-        name="serve",
-    )(asked.reshape(steps, per, 128), rows)
-
-
-def plan_kernel(a_ref, pos_ref, row_ref, start_ref, info_ref, key_ref, lv_ref, col_ref, acc_ref, end_ref):
+    wanted = (acc[:, :CAP] * 16.0 + acc[:, CAP:]).astype(I32) - 1
+    w_ref[...] = jnp.concatenate([wanted] + [jnp.full((chips, CAP), -1, I32)] * (128 // CAP - 1), axis=1)
+
+
+def plan_way_back(a, pos_ref, row_ref, start_ref, info_ref, key_ref, lv_ref, col_ref, acc_ref, end_ref):
     rows_dev = start_ref.shape[0]
-    nrow = a_ref.shape[0]
+    nrow = a.shape[0]
     slots = nrow * 128
-    a = a_ref[...]
     live = (a >= 0) & (a < rows_dev)
     sid = iota((nrow, 128), 0) * 128 + iota((nrow, 128), 1)
     key = jnp.where(live, a * slots + sid, (1 << 30) + sid)
@@ -188,12 +201,12 @@
         at = pl.ds(pl.multiple_of(g * 128, 128), 128)
         end_ref[at, :] = jnp.broadcast_to((start + count).astype(I32), (128, 128))
         start_ref[at, :] = jnp.broadcast_to(jnp.where(count > 0, start, -1.0).astype(I32), (128, 128))
-        return jnp.maximum(most, jnp.max(count))
-
-    most = lax.fori_loop(0, rows_dev // 128, start_of, jnp.float32(0))
-    total = jnp.sum(jnp.where(live, 1.0, 0.0)).astype(I32)
-    info_ref[0] = total
-    info_ref[1] = most.astype(I32)
+        return jnp.maximum(most, count)
+
+    most = lax.fori_loop(0, rows_dev // 128, start_of, jnp.zeros((128, 1), F32))
+    total = jnp.sum(jnp.where(live, 1.0, 0.0), axis=(0, 1), keepdims=True).astype(I32)
+    most = jnp.max(most, axis=0, keepdims=True).astype(I32)
+    info_ref[...] = jnp.where(iota((8, 128), 1) == 0, total, most)
     row_ref[...] = jnp.full(row_ref.shape, rows_dev, I32)
 
     def row_of(c, carry):
@@ -208,35 +221,161 @@
     lax.fori_loop(0, nrow, row_of, 0)
 
 
-def plan(asked_rows, rows_dev):
-    nrow = asked_rows.shape[0]
+def pull_kernel(
+    c_ref, emb_ref,
+    pulled_ref, slot_ref, pos_ref, row_ref, start_ref, info_ref,
+    rows_ref, served_ref, w_ref, d_ref, e_ref, fin_ref,
+    key_ref, lv_ref, col_ref, acc_ref, end_ref,
+    keep_sem, half_send, half_recv, col_send, col_recv, plane_send, plane_recv, out_send, out_recv, own_sem,
+):
+    here = place()
+    y, z, x, side = here
+    rows_dev = emb_ref.shape[0]
+    span = rows_ref.shape[0]
+    chips = pulled_ref.shape[0]
+    wait_for_peers = greet(here)
+    my_half = rows_ref.at[pl.ds(pl.multiple_of(side * rows_dev, rows_dev), rows_dev)]
+    keep = pltpu.make_async_copy(emb_ref, my_half, keep_sem)
+    keep.start()
+    slots_of(c_ref, w_ref, slot_ref, span.bit_length() - 1)
+    wait_for_peers()
+    half = remote(emb_ref, my_half, half_send, half_recv, {"rows": chip_at(y, z, x), "sub": 1 - side})
+    half.start()
+
+    copies = []
+    for dz, device in column_peers(here):
+        src = w_ref.at[pl.ds(pl.multiple_of(lax.rem(z + dz, NZ) * PLANE, PLANE), PLANE)]
+        dst = d_ref.at[pl.ds(far_rank(-dz) * PLANE, PLANE)]
+        copies.append(remote(src, dst, col_send.at[dz], col_recv.at[dz], device))
+        copies[-1].start()
+    own = pl.ds(pl.multiple_of(z * PLANE, PLANE), PLANE)
+    d_ref[far_rank(0) * PLANE : (far_rank(0) + 1) * PLANE, :] = w_ref[own, :]
+    for copy in copies:
+        copy.wait()
+    copies = []
+    for dy, dx, h, device in plane_peers(here):
+        i = plane_rank(dy, dx)
+        if h == 0 or i == 0:
+            cell = lax.rem(y + dy, NY) * NX + lax.rem(x + dx, NX)
+            e_ref[i * NZ : (i + 1) * NZ, :] = d_ref[pl.ds(cell, NZ, stride=PLANE), :]
+        at = h * chips + plane_rank(-dy, -dx) * NZ
+        copies.append(
+            remote(
+                e_ref.at[pl.ds(i * NZ, NZ)], fin_ref.at[pl.ds(at, NZ)],
+                plane_send.at[2 * i + h], plane_recv.at[2 * i + h], device,
+            )
+        )
+        copies[-1].start()
+    fin_ref[0:NZ, :] = e_ref[0:NZ, :]
+    for copy in copies:
+        copy.wait()
+    keep.wait()
+    half.wait()
+
+    spread = iota((128, 128), 1) == (iota((128, 128), 0) & (CAP - 1))
+    ids = iota((128, span), 1)
+    me = z * PLANE + y * NX + x
+
+    def serve(t, carry):
+        c = lax.rem(t + 1, PLANE)
+        asked = fin_ref[pl.ds(pl.multiple_of(c * NZ, NZ), NZ), :]
+        wide = jnp.concatenate([jnp.broadcast_to(asked[j : j + 1, :], (CAP, 128)) for j in range(NZ)], axis=0)
+        col = jnp.sum(jnp.where(spread, wide, 0), axis=1, keepdims=True)
+        got = dot(onehot(col == ids), rows_ref[...], NN).astype(BF16)
+        for j in range(NZ):
+            served_ref[c * NZ + j] = got[j * CAP : (j + 1) * CAP, :]
+        dy, dx = lax.div(c, NX), lax.rem(c, NX)
+
+        def send(j):
+            device = {"rows": chip_at(y + dy, z + FAR_FIRST[j], x + dx), "sub": side}
+            remote(served_ref.at[c * NZ + j], pulled_ref.at[me], out_send, out_recv, device).start()
+
+        for j in range(NZ - 1):
+            send(j)
+
+        @pl.when(c > 0)
+        def _():
+            send(NZ - 1)
+
+        return carry
+
+    lax.fori_loop(0, PLANE, serve, 0)
+    stay = pltpu.make_async_copy(served_ref.at[NZ - 1], pulled_ref.at[me], own_sem)
+    stay.start()
+
+    rows = [fin_ref[h * chips : (h + 1) * chips, :].T[0:CAP, :] for h in range(2)]
+    plan_way_back(
+        jnp.concatenate(rows, axis=0) - side * rows_dev,
+        pos_ref, row_ref, start_ref, info_ref, key_ref, lv_ref, col_ref, acc_ref, end_ref,
+    )
+    stay.wait()
+    rest = pl.ds(0, chips - 1)
+    pltpu.make_async_copy(served_ref.at[rest], served_ref.at[rest], out_send).wait()
+    pltpu.make_async_copy(pulled_ref.at[rest], pulled_ref.at[rest], out_recv).wait()
+
+
+def pull(candidates, embeddings, chips):
+    rows_dev, width = embeddings.shape
+    nrow = 2 * CAP
+    vmem = pl.BlockSpec(memory_space=pltpu.VMEM)
+    anywhere = pl.BlockSpec(memory_space=pl.ANY)
+    grid = pltpu.VMEM((chips, 128), I32)
+    dma = pltpu.SemaphoreType.DMA
     return pl.pallas_call(
-        plan_kernel,
+        pull_kernel,
+        in_specs=[vmem, anywhere],
+        out_specs=[vmem] * 6,
         out_shape=(
+            jax.ShapeDtypeStruct((chips, CAP, width), BF16),
+            jax.ShapeDtypeStruct(candidates.shape, I32),
             jax.ShapeDtypeStruct((nrow, 128), I32),
             jax.ShapeDtypeStruct((PITCH, 128), I32),
             jax.ShapeDtypeStruct((rows_dev, 128), I32),
-            jax.ShapeDtypeStruct((2,), I32),
-        ),
-        out_specs=(
-            pl.BlockSpec(memory_space=pltpu.VMEM),
-            pl.BlockSpec(memory_space=pltpu.VMEM),
-            pl.BlockSpec(memory_space=pltpu.VMEM),
-            pl.BlockSpec(memory_space=pltpu.SMEM),
+            jax.ShapeDtypeStruct((8, 128), I32),
         ),
         scratch_shapes=[
+            pltpu.VMEM((2 * rows_dev, width), BF16),
+            pltpu.VMEM((chips, CAP, width), BF16),
+            grid, grid, grid,
+            pltpu.VMEM((2 * chips, 128), I32),
             pltpu.VMEM((nrow, 128), I32),
             pltpu.VMEM((nrow, 128), I32),
             pltpu.VMEM((128, nrow), I32),
             pltpu.VMEM((nrow * 8, 128), F32),
             pltpu.VMEM((rows_dev, 128), I32),
+            dma, dma, dma, dma((NZ,)), dma((NZ,)), dma((2 * PLANE,)), dma((2 * PLANE,)), dma, dma, dma,
         ],
-        cost_estimate=pl.CostEstimate(flops=20_000_000_000, bytes_accessed=1_000_000, transcendentals=0),
-        name="plan",
-    )(asked_rows)
-
-
-def join_kernel(pulled_ref, own_ref, slot_ref, flag_ref, out_ref, fwd_ref, z_ref, f_ref, a_ref, t_ref, hot_ref, pay_ref):
+        compiler_params=pltpu.CompilerParams(
+            collective_id=0, has_side_effects=True, vmem_limit_bytes=40 << 20
+        ),
+        name="pull",
+    )(candidates, embeddings)
+
+
+def near(fwd_ref, cur_ref, out_ref, s_ref):
+    blocks = cur_ref.shape[0] // 128
+    for b in range(blocks):
+        s_ref[b * K : (b + 1) * K, :] = cur_ref[b * 128 : (b + 1) * 128, :].T
+    best = sort_list([s_ref[pl.ds(k, 8, stride=K), :] for k in range(K)])
+
+    def body(g, best):
+        more = [fwd_ref[pl.ds(g * K + t, 8, stride=128), :] for t in range(K)]
+        return tuple(merge_lists(list(best), sort_list(more)))
+
+    best = lax.fori_loop(0, 128 // K, body, tuple(best))
+    for k in range(K):
+        out_ref[k * 8 : (k + 1) * 8, :] = best[k]
+
+
+def join_kernel(
+    pulled_ref, own_ref, slot_ref, flag_ref, cur_ref,
+    back_ref, near_ref,
+    z_ref, f_ref, a_ref, t_ref, hot_ref, pay_ref, fwd_ref, w_ref, d_ref, s_ref,
+    col_send, col_recv, plane_send, plane_recv, own_sem,
+):
+    here = place()
+    y, z, x, side = here
+    wait_for_peers = greet(here)
     blocks = slot_ref.shape[0]
     slots = pulled_ref.shape[0]
     slot_cols = slot_ref[...].T
@@ -251,8 +390,8 @@
         pick = onehot(slot_cols[:, b : b + 1] == ids)
         z_ref[0:128, :] = own_ref[at, :]
         z_ref[128:256, :] = dot(pick, pulled_ref[...], NN).astype(BF16)
-        z = z_ref[...]
-        gram = dot(z, z, NT)
+        both = z_ref[...]
+        gram = dot(both, both, NT)
         diag = jnp.where(eye, gram, 0.0)
         n_col = jnp.sum(diag, axis=1, keepdims=True)
         n_row = jnp.sum(diag, axis=0, keepdims=True)
@@ -289,17 +428,49 @@
         pay_ref[128:256, at] = mid
         hot_ref[:, at] = onehot(lax.shift_right_logical(slot, 2) == groups)
     both = dot(hot_ref[...], pay_ref[...], NT)
-    out_ref[...] = both[:, 0:128] + both[:, 128:256]
-
-
-def join(pulled, own, slots, flags):
+    offers = both[:, 0:128] + both[:, 128:256]
+    per = CAP // 4
+    for n in range(slots // CAP):
+        w_ref[n] = offers[n * per : (n + 1) * per, :]
+    wait_for_peers()
+    copies = []
+    for dz, device in column_peers(here):
+        src = w_ref.at[pl.ds(lax.rem(z + dz, NZ) * PLANE, PLANE)]
+        copies.append(remote(src, d_ref.at[far_rank(-dz)], col_send.at[dz], col_recv.at[dz], device))
+        copies[-1].start()
+    stay = pltpu.make_async_copy(w_ref.at[pl.ds(z * PLANE, PLANE)], d_ref.at[far_rank(0)], own_sem)
+    stay.start()
+    near(fwd_ref, cur_ref, near_ref, s_ref)
+    stay.wait()
+    for copy in copies:
+        copy.wait()
+    copies = []
+    for dy, dx, h, device in plane_peers(here):
+        i = plane_rank(dy, dx)
+        cell = lax.rem(y + dy, NY) * NX + lax.rem(x + dx, NX)
+        dst = back_ref.at[h, plane_rank(-dy, -dx)]
+        copies.append(remote(d_ref.at[:, cell], dst, plane_send.at[2 * i + h], plane_recv.at[2 * i + h], device))
+        copies[-1].start()
+    stay = pltpu.make_async_copy(d_ref.at[:, y * NX + x], back_ref.at[0, 0], own_sem)
+    stay.start()
+    stay.wait()
+    for copy in copies:
+        copy.wait()
+
+
+def join(pulled, own, slots, flags, current):
     n = pulled.shape[0]
     rows, width = own.shape
+    vmem = pl.BlockSpec(memory_space=pltpu.VMEM)
+    dma = pltpu.SemaphoreType.DMA
+    per = CAP // 4
     return pl.pallas_call(
         join_kernel,
+        in_specs=[vmem] * 5,
+        out_specs=[vmem] * 2,
         out_shape=(
-            jax.ShapeDtypeStruct((n // 4, 128), F32),
-            jax.ShapeDtypeStruct((rows, 128), F32),
+            jax.ShapeDtypeStruct((2, PLANE, NZ, per, 128), F32),
+            jax.ShapeDtypeStruct((K * 8, 128), F32),
         ),
         scratch_shapes=[
             pltpu.VMEM((256, width), BF16),
@@ -308,50 +479,32 @@
             pltpu.VMEM((K * 8, 128), F32),
             pltpu.VMEM((n // 4, rows), BF16),
             pltpu.VMEM((256, rows), BF16),
+            pltpu.VMEM((rows, 128), F32),
+            pltpu.VMEM((n // CAP, per, 128), F32),
+            pltpu.VMEM((NZ, PLANE, per, 128), F32),
+            pltpu.VMEM((rows // 128 * K, 128), F32),
+            dma((NZ,)), dma((NZ,)), dma((2 * PLANE,)), dma((2 * PLANE,)), dma,
         ],
-        compiler_params=pltpu.CompilerParams(vmem_limit_bytes=40 << 20),
+        compiler_params=pltpu.CompilerParams(
+            collective_id=1, has_side_effects=True, vmem_limit_bytes=40 << 20
+        ),
         name="join",
-    )(pulled, own, slots, flags)
-
-
-def near_kernel(fwd_ref, cur_ref, out_ref, s_ref):
-    blocks = cur_ref.shape[0] // 128
-    for b in range(blocks):
-        s_ref[b * K : (b + 1) * K, :] = cur_ref[b * 128 : (b + 1) * 128, :].T
-    best = sort_list([s_ref[pl.ds(k, 8, stride=K), :] for k in range(K)])
-
-    def body(g, best):
-        more = [fwd_ref[pl.ds(g * K + t, 8, stride=128), :] for t in range(K)]
-        return tuple(merge_lists(list(best), sort_list(more)))
-
-    best = lax.fori_loop(0, 128 // K, body, tuple(best))
-    for k in range(K):
-        out_ref[k * 8 : (k + 1) * 8, :] = best[k]
-
-
-def near(fwd, current):
-    return pl.pallas_call(
-        near_kernel,
-        out_shape=jax.ShapeDtypeStruct((K * 8, 128), F32),
-        scratch_shapes=[pltpu.VMEM((current.shape[0] // 128 * K, 128), F32)],
-        cost_estimate=pl.CostEstimate(flops=8_000_000_000, bytes_accessed=1_000_000, transcendentals=0),
-        name="near",
-    )(fwd, current)
-
-
-def merge_kernel(mine_ref, his_ref, pos_ref, row_ref, start_ref, info_ref, near_ref, out_ref, pay_ref, s_ref, x_ref, acc_ref):
-    half = mine_ref.shape[0]
+    )(pulled, own, slots, flags, current)
+
+
+def merge_kernel(back_ref, pos_ref, row_ref, start_ref, info_ref, near_ref, out_ref, pay_ref, s_ref, x_ref, acc_ref):
     rows_dev = out_ref.shape[0]
-    lanes = iota((half, 128), 1)
+    group = lax.shift_right_logical(iota((128, 128), 1), 5)
     total = info_ref[0]
     most = info_ref[1]
-    for h, ref in enumerate((mine_ref, his_ref)):
-        vals = ref[...]
-        for q in range(4):
-            at = slice((q * 2 + h) * half, (q * 2 + h + 1) * half)
-            hi, mid = split2(jnp.where(lax.shift_right_logical(lanes, 5) == q, vals, 0.0))
-            pay_ref[at, 0:128] = hi
-            pay_ref[at, 128:256] = mid
+    for h in range(2):
+        for rr in range(CAP // 4):
+            vals = back_ref[h, :, rr, :]
+            for q in range(4):
+                n = (h * CAP + rr * 4 + q) * 128
+                hi, mid = split2(jnp.where(group == q, vals, 0.0))
+                pay_ref[n : n + 128, 0:128] = hi
+                pay_ref[n : n + 128, 128:256] = mid
     s_ref[...] = jnp.full(s_ref.shape, FAR, F32)
     chunks = (total + 127) // 128
     width = pay_ref.shape[0]
@@ -421,12 +574,12 @@
         out_ref[b * 128 : (b + 1) * 128, :] = x_ref[pl.ds(b, K, stride=8), :].T
 
 
-def merge(mine, his, pos, row, start, info, best):
+def merge(back, pos, row, start, info, best):
     rows_dev = start.shape[0]
     vmem = pl.BlockSpec(memory_space=pltpu.VMEM)
     return pl.pallas_call(
         merge_kernel,
-        in_specs=[vmem] * 5 + [pl.BlockSpec(memory_space=pltpu.SMEM), vmem],
+        in_specs=[vmem] * 4 + [pl.BlockSpec(memory_space=pltpu.SMEM), vmem],
         out_specs=vmem,
         out_shape=jax.ShapeDtypeStruct((rows_dev, K), F32),
         scratch_shapes=[
@@ -437,34 +590,16 @@
         ],
         compiler_params=pltpu.CompilerParams(vmem_limit_bytes=40 << 20),
         name="merge",
-    )(mine, his, pos, row, start, info, best)
+    )(back, pos, row, start, info, best)
 
 
 def per_device(embeddings, candidates, fresh_flags, current):
-    rows_dev = embeddings.shape[0]
     chips = lax.axis_size("rows")
-    sides = lax.axis_size("sub")
-    swap = [(i, i ^ 1) for i in range(sides)]
-    span = sides * rows_dev
-    total = chips * CAP
-    wanted, slots = layout(candidates, chips, span)
-    chip_rows = lax.all_gather(embeddings, "sub", axis=0, tiled=True)
-    asked = lax.all_to_all(wanted, "rows", split_axis=0, concat_axis=0, tiled=True)
-    served = serve(asked.reshape(total // 128, 128), chip_rows)
-    pulled = lax.all_to_all(
-        served.reshape(chips, CAP, -1), "rows", split_axis=0, concat_axis=0, tiled=True
-    ).reshape(total, -1)
-    his_asked = lax.ppermute(asked, "sub", swap)
-    here = jnp.stack([asked, his_asked]) - lax.axis_index("sub") * rows_dev
-    here = here.reshape(2, chips, CAP // 4, 4).transpose(3, 0, 1, 2).reshape(-1, 128)
-    pos, row, start, info = plan(here, rows_dev)
-    outgoing, fwd = join(pulled, embeddings, slots, fresh_flags)
-    returned = lax.all_to_all(
-        outgoing.reshape(chips, CAP // 4, 128), "rows", split_axis=0, concat_axis=0, tiled=True
-    ).reshape(total // 4, 128)
-    best = near(fwd, current)
-    his = lax.ppermute(returned, "sub", swap)
-    return merge(returned, his, pos.reshape(1, -1), row, start, info, best)
+    pulled, slots, pos, row, start, info = pull(candidates, embeddings, chips)
+    pulled = pulled.reshape(chips * CAP, -1)
+    back, best = join(pulled, embeddings, slots, fresh_flags, current)
+    back = back.reshape(2, chips, CAP // 4, 128)
+    return merge(back, pos.reshape(1, -1), row, start, info[0, 0:2], best)
 
 
 def solution(mesh):

time: 204 us -> 130 us (0.64)
  waiting for transfers between devices: 66.8 us -> 0 us
  Pallas kernels: 62.4 us -> 124 us
  blocking collectives: 26.8 us -> 0 us
  starting transfers between devices: 20.5 us -> 0 us
  between operations: 13.5 us -> 0.06 us
  local copies, waits for them, and re-layouts: 12 us -> 6.11 us
    all_to_all x2 -> x0, waiting for transfers between devices: 66.1 us -> none  [the longest x1 66.1 us: per_device(): lax.all_to_all(served.reshape(chips, CAP, -1), 'rows', split_axis=0, conc...]
    pallas_call x6 -> x3, Pallas kernels: 62.4 us -> 124 us  [the longest x1 91.2 us: pull(): pl.pallas_call(pull_kernel, in_specs=[vmem, anywhere], out_specs=[vmem] *...]
    all_to_all x1 -> x0, blocking collectives: 26.8 us -> none  [per_device(): lax.all_to_all(wanted, 'rows', split_axis=0, concat_axis=0, tiled=True)]
    all_to_all x2 -> x0, starting transfers between devices: 17.6 us -> none  [the longest x1 10.1 us: per_device(): lax.all_to_all(outgoing.reshape(chips, CAP // 4, 128), 'rows', split_axis...]
    ppermute x2 -> x0, starting transfers between devices: 2.9 us -> none  [the longest x1 1.72 us: per_device(): his = lax.ppermute(returned, 'sub', swap)]
    unnamed x25 -> x9, local copies, waits for them, and re-layouts: 7.64 us -> 5.28 us
  transfers between devices with their start and end apart: 5 -> 0, of which waited for: 1 -> 0; matrix products, arithmetic and copies ran while one was open for 3% -> 0% of each run, Pallas kernels for 19% -> 0%
where the time goes in v2:
time: 130 us
  Pallas kernels  124 us (95%)
  local copies, waits for them, and re-layouts  6.11 us (5%)
    pallas_call x1, Pallas kernels, pull(): pl.pallas_call(pull_kernel, in_specs=[vmem, anywhere], out_specs=[vmem] *...  91.2 us
    pallas_call x1, Pallas kernels, join(): pl.pallas_call(join_kernel, in_specs=[vmem] * 5, out_specs=[vmem] * 2, ou...  24.7 us
    pallas_call x1, Pallas kernels, merge(): pl.pallas_call(merge_kernel, in_specs=[vmem] * 4 + [pl.BlockSpec(memory_s...  7.86 us
    unnamed x9, local copies, waits for them, and re-layouts  5.28 us

profile of v2, /device:TPU:1, one launch (start us, length us, event | category | flops | bytes accessed | tf_op | source)
XLA Modules:
  0.0 129.9 jit_solution(15101448127428152137)
XLA Ops:
  0.0 1.1 copy.5.cur_ref
  1.1 0.0 copy-start
  1.1 1.4 %copy-done = bf16[1024,768]{1,0:T(8,128)(2,1)S(1)} copy-done((bf16[1024,768]{1,0:T(8,128)(2,1)S(1)}, bf16[1024,768]{1,0:T(8,128)(2,1)}, u32[]{:S(2)}) %copy-start) | copy-done | bytes 1572888
  2.5 0.0 copy-start.2
  2.5 0.7 copy-done.2
  3.2 91.2 %pull.1 = (bf16[128,16,768]{2,1,0:T(8,128)(2,1)S(1)}, s32[8,128]{1,0:T(8,128)S(1)}, s32[32,128]{1,0:T(8,128)S(1)}, s32[40,128]{1,0:T(8,128)S(1)}, s32[1024,128]{1,0:T(8,128)S(1)}, /*index=5*/s32[8,128]{1,0:T(8,128)S(1)}) custom-call(s32[8,128]{1,0:T(8,128)S(1)} %copy-done.2, bf16[1024,768]{1,0:T(8,128)(2,1)S(1)} %copy-done), custom_call_target="tpu_custom_call" | custom-call | tf_op jit(solution)/shard_map/pull/pallas_call | solution.py:324
  94.4 0.0 copy-start.1
  94.4 1.4 %copy-done.1 = bf16[1024,768]{1,0:T(8,128)(2,1)S(1)} copy-done((bf16[1024,768]{1,0:T(8,128)(2,1)S(1)}, bf16[1024,768]{1,0:T(8,128)(2,1)}, u32[]{:S(2)}) %copy-start.1) | copy-done | bytes 1572888
  95.8 0.0 copy-start.3
  95.8 0.7 copy-done.3
  96.5 24.7 %join.1 = (f32[2,16,8,4,128]{4,3,2,1,0:T(4,128)S(1)}, f32[256,128]{1,0:T(8,128)S(1)}) custom-call(bf16[2048,768]{1,0:T(8,128)(2,1)S(1)} %bitcast.5, bf16[1024,768]{1,0:T(8,128)(2,1)S(1)} %copy-done.1, s32[8,128]{1,0:T(8,128)S(1)} %get-tuple-element.14.slot_ref, s32[8,128]{1,0:T(8,128)S(1)} %copy-done.3, f32[1024,32]{1,0:T(8,128)S(1)} %copy.5.cur_ref), custom_call_target="tpu_custom_call" | custom-call | tf_op jit(solution)/shard_map/join/pallas_call | solution.py:467
  121.2 7.9 %merge.1 = f32[1024,32]{1,0:T(8,128)S(1)} custom-call(f32[2,128,4,128]{3,2,1,0:T(4,128)S(1)} %bitcast.6, s32[1,4096]{1,0:T(1,128)S(1)} %bitcast.7, s32[40,128]{1,0:T(8,128)S(1)} %get-tuple-element.17.row_ref, s32[1024,128]{1,0:T(8,128)S(1)} %get-tuple-element.18.start_ref, s32[2]{0:T(128)S(1)} %slice_bitcast_fusion.info_ref, ...), custom_call_target="tpu_custom_call" | custom-call | tf_op jit(solution)/shard_map/merge/pallas_call | solution.py:580
  129.1 0.8 copy.6
  (1 shorter events, 0.0 us)
Async XLA Ops:
  1.1 1.4 %copy-start = (bf16[1024,768]{1,0:T(8,128)(2,1)S(1)}, bf16[1024,768]{1,0:T(8,128)(2,1)}, u32[]{:S(2)}) copy-start(bf16[1024,768]{1,0:T(8,128)(2,1)} %own_ref.1) | copy-start | bytes 4718596
  2.5 0.7 copy-start.2
  94.4 1.4 %copy-start.1 = (bf16[1024,768]{1,0:T(8,128)(2,1)S(1)}, bf16[1024,768]{1,0:T(8,128)(2,1)}, u32[]{:S(2)}) copy-start(bf16[1024,768]{1,0:T(8,128)(2,1)} %own_ref.1) | copy-start | bytes 4718596
  95.8 0.7 copy-start.3

commit v3 on v2

v3 whole, which is shorter than its diff:
```python
import functools

import jax
import jax.numpy as jnp
from jax import lax
from jax.experimental import pallas as pl
from jax.experimental.pallas import tpu as pltpu
from jax.sharding import PartitionSpec as P

BLOCK = 128
CAP = 16
K = 32
FAR = 1.0e9
F32, BF16, I32 = jnp.float32, jnp.bfloat16, jnp.int32
NT = (((1,), (1,)), ((), ()))
NN = (((1,), (0,)), ((), ()))
PITCH = 40
NY, NZ, NX = 4, 8, 4
PLANE = NY * NX
AWAY = (0, 4, 3, 5, 2, 6, 1, 7)
STEP = 384
READY = 3
SCALE = 28672.0
TOP = 65535.0
MESH = pl.DeviceIdType.MESH


def dot(a, b, dims):
    return lax.dot_general(a, b, dims, preferred_element_type=F32)


def sort_pairs(n):
    pairs = []
    p = 1
    while p < n:
        k = p
        while k >= 1:
            for j in range(k % p, n - k, 2 * k):
                for i in range(min(k, n - j - k)):
                    if (i + j) // (2 * p) == (i + j + k) // (2 * p):
                        pairs.append((i + j, i + j + k))
            k //= 2
        p *= 2
    return pairs


SORT = sort_pairs(K)


def exchange(v, i, j):
    v[i], v[j] = jnp.minimum(v[i], v[j]), jnp.maximum(v[i], v[j])


def sort_list(values):
    v = list(values)
    for i, j in SORT:
        exchange(v, i, j)
    return v


def merge_low(mins):
    v = list(mins)
    d = K // 2
    while d >= 1:
        for i in range(K):
            if i & d == 0:
                exchange(v, i, i + d)
        d //= 2
    return v


def merge_lists(a, b):
    return merge_low([jnp.minimum(a[i], b[K - 1 - i]) for i in range(K)])


def split2(x):
    hi = x.astype(BF16)
    mid = (x - hi.astype(F32)).astype(BF16)
    return hi, mid


def iota(shape, dim):
    return lax.broadcasted_iota(I32, shape, dim)


def onehot(mask):
    return jnp.where(mask, 1.0, 0.0).astype(BF16)


def place():
    chip = lax.axis_index("rows")
    return lax.div(chip, NZ * NX), lax.rem(lax.div(chip, NX), NZ), lax.rem(chip, NX), lax.axis_index("sub")


def chip_at(y, z, x):
    return (lax.rem(y, NY) * NZ + lax.rem(z, NZ)) * NX + lax.rem(x, NX)


def column_peers(here):
    y, z, x, side = here
    return [(dz, {"rows": chip_at(y, z + dz, x), "sub": side}) for dz in AWAY[1:]]


def plane_peers(here):
    y, z, x, side = here
    return [
        (dy, dx, h, {"rows": chip_at(y + dy, z, x + dx), "sub": lax.rem(side + h, 2)})
        for dy in range(NY)
        for dx in range(NX)
        for h in range(2)
        if dy + dx + h > 0
    ]


def greet(here):
    sem = pltpu.get_barrier_semaphore()
    peers = [p[-1] for p in column_peers(here)] + [p[-1] for p in plane_peers(here)]
    for device in peers:
        pl.semaphore_signal(sem, inc=1, device_id=device, device_id_type=MESH)
    return lambda: pl.semaphore_wait(sem, len(peers))


def remote(src, dst, send, recv, device):
    return pltpu.make_async_remote_copy(
        src_ref=src, dst_ref=dst, send_sem=send, recv_sem=recv, device_id=device, device_id_type=MESH
    )


def away(k):
    m = k - 1
    dz = jnp.where(lax.rem(m, 2) == 1, 4 - lax.div(m + 1, 2), 4 + lax.div(m, 2))
    return jnp.where(k == 0, 0, dz)


def far_rank(dz):
    return AWAY.index(dz % NZ)


def plane_rank(dy, dx):
    return (dy % NY) * NX + dx % NX


def slots_of(c_ref, w_ref, s_ref, span_bits):
    blocks, n = c_ref.shape
    chips = w_ref.shape[0]
    owners = iota((chips, n), 0)
    before = onehot(iota((n, n), 0) < iota((n, n), 1))
    ranks = iota((CAP, n), 0)
    run = jnp.zeros((chips, 1), F32)
    acc = jnp.zeros((chips, 2 * CAP), F32)
    for b in range(blocks):
        c = c_ref[b : b + 1, :]
        chip = lax.shift_right_logical(c, span_bits)
        owner = (chip & 28) * 4 + lax.shift_right_logical(chip, 5) * 4 + (chip & 3)
        row1 = (c & ((1 << span_bits) - 1)) + 1
        mine = owner == owners
        mine_b = onehot(mine)
        pre = dot(mine_b, before, NN) + run
        rank = jnp.sum(jnp.where(mine, pre, 0.0), axis=0, keepdims=True).astype(I32)
        run = run + jnp.sum(jnp.where(mine, 1.0, 0.0), axis=1, keepdims=True)
        s_ref[b : b + 1, :] = owner * CAP + rank
        sel = ranks == rank
        hi = jnp.where(sel, lax.shift_right_logical(row1, 4).astype(F32), 0.0).astype(BF16)
        lo = jnp.where(sel, (row1 & 15).astype(F32), 0.0).astype(BF16)
        acc = acc + dot(mine_b, jnp.concatenate([hi, lo], axis=0), NT)
    wanted = (acc[:, :CAP] * 16.0 + acc[:, CAP:]).astype(I32) - 1
    w_ref[...] = jnp.concatenate([wanted] + [jnp.full((chips, CAP), -1, I32)] * (128 // CAP - 1), axis=1)


def plan_way_back(a, pos_ref, row_ref, start_ref, info_ref, key_ref, lv_ref, col_ref, acc_ref, end_ref):
    rows_dev = start_ref.shape[0]
    nrow = a.shape[0]
    slots = nrow * 128
    live = (a >= 0) & (a < rows_dev)
    sid = iota((nrow, 128), 0) * 128 + iota((nrow, 128), 1)
    key = jnp.where(live, a * slots + sid, (1 << 30) + sid)
    key_ref[...] = key
    lv_ref[...] = jnp.where(live, a, rows_dev)
    for h in range(nrow // 8):
        col_ref[:, h * 8 : (h + 1) * 8] = key[h * 8 : (h + 1) * 8, :].T
    acc_ref[...] = jnp.zeros_like(acc_ref)
    lane = iota((128, nrow), 1)

    def outer(c, carry):
        col = jnp.sum(jnp.where(lane == c, col_ref[...], 0), axis=1, keepdims=True)
        colb = jnp.broadcast_to(col, (128, 128))

        def inner(e, carry):
            less = jnp.where(colb < key_ref[pl.ds(e, 1), :], 1.0, 0.0)
            part = jnp.sum(less.reshape(16, 8, 128), axis=0)
            at = pl.ds(pl.multiple_of(e * 8, 8), 8)
            acc_ref[at, :] = acc_ref[at, :] + part
            return carry

        return lax.fori_loop(0, nrow, inner, carry)

    lax.fori_loop(0, nrow, outer, 0)
    for e in range(nrow):
        pos_ref[e : e + 1, :] = jnp.sum(acc_ref[e * 8 : (e + 1) * 8, :], axis=0, keepdims=True).astype(I32)

    def start_of(g, most):
        v = g * 128 + iota((128, 128), 0)
        low = jnp.zeros((128, 128), F32)
        own = jnp.zeros((128, 128), F32)
        for e in range(nrow):
            lv = lv_ref[e : e + 1, :]
            low = low + jnp.where(lv < v, 1.0, 0.0)
            own = own + jnp.where(lv == v, 1.0, 0.0)
        start = jnp.sum(low, axis=1, keepdims=True)
        count = jnp.sum(own, axis=1, keepdims=True)
        at = pl.ds(pl.multiple_of(g * 128, 128), 128)
        end_ref[at, :] = jnp.broadcast_to((start + count).astype(I32), (128, 128))
        start_ref[at, :] = jnp.broadcast_to(jnp.where(count > 0, start, -1.0).astype(I32), (128, 128))
        return jnp.maximum(most, count)

    most = lax.fori_loop(0, rows_dev // 128, start_of, jnp.zeros((128, 1), F32))
    total = jnp.sum(jnp.where(live, 1.0, 0.0), axis=(0, 1), keepdims=True).astype(I32)
    most = jnp.max(most, axis=0, keepdims=True).astype(I32)
    info_ref[...] = jnp.where(iota((8, 128), 0) == 0, total, most).astype(F32)
    row_ref[...] = jnp.full(row_ref.shape, rows_dev, I32)

    def row_of(c, carry):
        p = c * 128 + iota((8, 128), 1)
        acc = jnp.zeros((8, 128), F32)
        for g in range(rows_dev // 8):
            acc = acc + jnp.where(end_ref[g * 8 : (g + 1) * 8, :] <= p, 1.0, 0.0)
        row = jnp.sum(acc, axis=0, keepdims=True).astype(I32)
        row_ref[pl.ds(c, 1), :] = jnp.where(p[0:1, :] < total, row, rows_dev)
        return carry

    lax.fori_loop(0, nrow, row_of, 0)


def near(fwd_ref, cur_ref, out_ref, s_ref):
    for b in range(cur_ref.shape[1] // 128):
        s_ref[b * K : (b + 1) * K, :] = cur_ref[:, b * 128 : (b + 1) * 128]
    best = sort_list([s_ref[pl.ds(k, 8, stride=K), :] for k in range(K)])

    def body(g, best):
        more = [fwd_ref[pl.ds(g * K + t, 8, stride=128), :] for t in range(K)]
        return tuple(merge_lists(list(best), sort_list(more)))

    best = lax.fori_loop(0, 128 // K, body, tuple(best))
    for k in range(K):
        out_ref[k * 8 : (k + 1) * 8, :] = best[k]


def round_kernel(
    cand_hbm, flag_hbm, emb_hbm, cur_hbm,
    back_ref, near_ref, pos_ref, row_ref, info_ref, q_ref, start_ref, hit_ref,
    c_ref, flag_ref, cur_ref, slot_ref,
    rows_ref, served_ref, pulled_ref, w_ref, d_ref, e_ref, fin_ref, ask_ref,
    key_ref, lv_ref, col_ref, acc_ref, end_ref,
    cand_ref, z_ref, f_ref, a_ref, fwd_ref, t_ref, hot_ref, pay_ref, w2_ref, d2_ref, s_ref,
    in_sem, half_send, half_recv, col_send, col_recv, plane_send, plane_recv,
    out_send, out_recv, own_sem, col_send2, col_recv2, plane_send2, plane_recv2,
):
    here = place()
    y, z, x, side = here
    rows_dev = emb_hbm.shape[0]
    span = rows_ref.shape[0]
    chips = pulled_ref.shape[0]
    half_at = pl.multiple_of(side * rows_dev, rows_dev)
    my_half = rows_ref.at[pl.ds(half_at, rows_dev)]
    brought = [
        pltpu.make_async_copy(src, dst, in_sem.at[i])
        for i, (src, dst) in enumerate(
            [(cand_hbm, c_ref), (emb_hbm, my_half), (flag_hbm, flag_ref), (cur_hbm, cur_ref)]
        )
    ]
    for copy in brought:
        copy.start()
    wait_for_peers = greet(here)
    brought[0].wait()
    slots_of(c_ref, w_ref, slot_ref, span.bit_length() - 1)
    wait_for_peers()

    copies = []
    for dz, device in column_peers(here):
        src = w_ref.at[pl.ds(pl.multiple_of(lax.rem(z + dz, NZ) * PLANE, PLANE), PLANE)]
        dst = d_ref.at[pl.ds(far_rank(-dz) * PLANE, PLANE)]
        copies.append(remote(src, dst, col_send.at[dz], col_recv.at[dz], device))
        copies[-1].start()
    half = remote(emb_hbm, my_half, half_send, half_recv, {"rows": chip_at(y, z, x), "sub": 1 - side})
    half.start()
    own = pl.ds(pl.multiple_of(z * PLANE, PLANE), PLANE)
    d_ref[far_rank(0) * PLANE : (far_rank(0) + 1) * PLANE, :] = w_ref[own, :]
    for copy in copies:
        copy.wait()
    copies = []
    for dy, dx, h, device in plane_peers(here):
        i = plane_rank(dy, dx)
        if h == 0 or i == 0:
            cell = lax.rem(y + dy, NY) * NX + lax.rem(x + dx, NX)
            e_ref[i * NZ : (i + 1) * NZ, :] = d_ref[pl.ds(cell, NZ, stride=PLANE), :]
        at = h * chips + plane_rank(-dy, -dx) * NZ
        copies.append(
            remote(
                e_ref.at[pl.ds(i * NZ, NZ)], fin_ref.at[pl.ds(at, NZ)],
                plane_send.at[2 * i + h], plane_recv.at[2 * i + h], device,
            )
        )
        copies[-1].start()
    fin_ref[0:NZ, :] = e_ref[0:NZ, :]
    for copy in copies:
        copy.wait()
    for k in range(NZ):
        ask_ref[k * PLANE : (k + 1) * PLANE, :] = fin_ref[pl.ds(k, PLANE, stride=NZ), :]
    for copy in brought[1:]:
        copy.wait()
    half.wait()

    spread = iota((128, 128), 1) == (iota((128, 128), 0) & (CAP - 1))
    ids = iota((128, span), 1)
    me = z * PLANE + y * NX + x
    part = PLANE // 2

    def serve(t, carry):
        asked = ask_ref[pl.ds(pl.multiple_of(t * part, part), part), :]
        wide = jnp.concatenate([jnp.broadcast_to(asked[j : j + 1, :], (CAP, 128)) for j in range(part)], axis=0)
        col = jnp.sum(jnp.where(spread, wide, 0), axis=1, keepdims=True)
        got = dot(onehot(col == ids), rows_ref[...], NN).astype(BF16)
        for j in range(part):
            served_ref[t * part + j] = got[j * CAP : (j + 1) * CAP, :]
        k = lax.div(t, 2)
        dz = away(k)

        def send(j):
            i = lax.rem(t, 2) * part + j
            device = {"rows": chip_at(y + lax.div(i, NX), z + dz, x + lax.rem(i, NX)), "sub": side}
            remote(served_ref.at[t * part + j], pulled_ref.at[me], out_send, out_recv.at[k], device).start()

        @pl.when(t > 0)
        def _():
            send(0)

        for j in range(1, part):
            send(j)
        return carry

    lax.fori_loop(0, 2 * NZ, serve, 0)
    stay = pltpu.make_async_copy(served_ref.at[0], pulled_ref.at[me], own_sem)
    stay.start()

    turned = [fin_ref[h * chips : (h + 1) * chips, :].T[0:CAP, :] for h in range(2)]
    plan_way_back(
        jnp.concatenate(turned, axis=0) - side * rows_dev,
        pos_ref, row_ref, start_ref, info_ref, key_ref, lv_ref, col_ref, acc_ref, end_ref,
    )

    def ready(t, carry):
        p = iota((128, 128), 0) + t * 128
        for e in range(pos_ref.shape[0]):
            q_ref[pl.ds(pl.multiple_of(t * 128, 128), 128), e * 128 : (e + 1) * 128] = onehot(pos_ref[e : e + 1, :] == p)
        return carry

    lax.fori_loop(0, READY * STEP // 128, ready, 0)
    for t in range(READY):
        for i in range(STEP // 128):
            p = iota((rows_dev, 128), 1) + (t * STEP + i * 128)
            hit_ref[t, :, i * 128 : (i + 1) * 128] = onehot(start_ref[...] == p)

    slot_cols = slot_ref[...].T
    blocks = slot_ref.shape[0]
    size = PLANE * CAP

    def arrived(k, count):
        got = pulled_ref.at[pl.ds(0, count)]
        pltpu.make_async_copy(got, got, out_recv.at[k]).wait()
        return lax.rem(z - away(k) + NZ, NZ)

    def picked(b, plane, rows):
        pick = onehot(slot_cols[:, b : b + 1] - plane * size == iota((128, size), 1))
        return dot(pick, rows, NN)

    def plane_rows(plane):
        return pulled_ref[pl.ds(plane * PLANE, PLANE)].reshape(size, -1)

    stay.wait()
    plane = arrived(0, PLANE - 1)
    rows = plane_rows(plane)
    for b in range(blocks):
        cand_ref[b * 128 : (b + 1) * 128, :] = picked(b, plane, rows)

    def more_rows(k, carry):
        plane = arrived(k, PLANE)
        rows = plane_rows(plane)
        for b in range(blocks):
            at = slice(b * 128, (b + 1) * 128)
            cand_ref[at, :] = cand_ref[at, :] + picked(b, plane, rows)
        return carry

    lax.fori_loop(1, NZ - 1, more_rows, 0)
    plane = arrived(NZ - 1, PLANE)
    rows = plane_rows(plane)

    flags = flag_ref[...]
    flag_cols = flags.T
    eye = iota((256, 256), 0) == iota((256, 256), 1)
    off_diag = iota((128, 128), 0) != iota((128, 128), 1)
    for b in range(blocks):
        at = slice(b * 128, (b + 1) * 128)
        z_ref[0:128, :] = rows_ref[pl.ds(half_at + b * 128, 128), :]
        z_ref[128:256, :] = (cand_ref[at, :] + picked(b, plane, rows)).astype(BF16)
        both = z_ref[...]
        gram = dot(both, both, NT)
        diag = jnp.where(eye, gram, 0.0)
        n_col = jnp.sum(diag, axis=1, keepdims=True)
        n_row = jnp.sum(diag, axis=0, keepdims=True)
        dist = n_col + n_row - 2.0 * gram
        f_ref[at, :] = dist[0:128, 128:256]
        fwd_ref[at, :] = dist[128:256, 0:128]
        fresh = (flag_cols[:, b : b + 1] + flags[b : b + 1, :]) > 0
        a_ref[at, :] = jnp.where(fresh & off_diag, dist[128:256, 128:256], FAR)

    def take(ref, g):
        return [ref[pl.ds(g * K + t, 8, stride=128), :] for t in range(K)]

    best = sort_list(take(f_ref, 0))

    def more(ref, lo, best):
        def body(g, best):
            return tuple(merge_lists(list(best), sort_list(take(ref, g))))

        return lax.fori_loop(lo, 128 // K, body, tuple(best))

    best = more(f_ref, 1, best)
    best = more(a_ref, 0, best)

    for k in range(K):
        t_ref[k * 8 : (k + 1) * 8, :] = jnp.floor(jnp.clip(best[k] * SCALE + 0.5, 0.0, TOP))
    octet = lax.shift_right_logical(iota((128, 128), 0), 4)
    groups = iota((chips * 2, 128), 0)
    for b in range(blocks):
        at = slice(b * 128, (b + 1) * 128)
        slot = slot_ref[b : b + 1, :]
        code = t_ref[pl.ds(b, K, stride=8), :]
        hi = jnp.floor(code * (1.0 / 256.0))
        lo = code - hi * 256.0
        mine = (slot & 7) == octet
        for i, piece in enumerate((hi[:16], lo[:16], hi[16:], lo[16:])):
            pay_ref[i * 128 : (i + 1) * 128, at] = jnp.where(mine, jnp.concatenate([piece] * 8, axis=0), 0.0).astype(BF16)
        hot_ref[:, at] = onehot(lax.shift_right_logical(slot, 3) == groups)
    sums = dot(hot_ref[...], pay_ref[...], NT)
    low = (sums[:, 0:128] * 256.0 + sums[:, 128:256]).astype(I32)
    high = (sums[:, 256:384] * 256.0 + sums[:, 384:512]).astype(I32)
    words = low + lax.shift_left(high, 16)
    for n in range(chips):
        w2_ref[n] = words[2 * n : 2 * n + 2, :]
    copies = []
    for dz, device in column_peers(here):
        src = w2_ref.at[pl.ds(lax.rem(z + dz, NZ) * PLANE, PLANE)]
        copies.append(remote(src, d2_ref.at[far_rank(-dz)], col_send2.at[dz], col_recv2.at[dz], device))
        copies[-1].start()
    stay = pltpu.make_async_copy(w2_ref.at[pl.ds(z * PLANE, PLANE)], d2_ref.at[far_rank(0)], own_sem)
    stay.start()
    near(fwd_ref, cur_ref, near_ref, s_ref)
    stay.wait()
    for copy in copies:
        copy.wait()
    copies = []
    for dy, dx, h, device in plane_peers(here):
        i = plane_rank(dy, dx)
        cell = lax.rem(y + dy, NY) * NX + lax.rem(x + dx, NX)
        dst = back_ref.at[h, plane_rank(-dy, -dx)]
        copies.append(remote(d2_ref.at[:, cell], dst, plane_send2.at[2 * i + h], plane_recv2.at[2 * i + h], device))
        copies[-1].start()
    stay = pltpu.make_async_copy(d2_ref.at[:, y * NX + x], back_ref.at[0, 0], own_sem)
    stay.start()
    stay.wait()
    for copy in copies:
        copy.wait()
    sent = served_ref.at[pl.ds(0, chips - 1)]
    pltpu.make_async_copy(sent, sent, out_send).wait()


def one_round(candidates, flags, embeddings, current, chips):
    rows_dev, width = embeddings.shape
    nrow = 2 * CAP
    vmem = pl.BlockSpec(memory_space=pltpu.VMEM)
    hbm = pl.BlockSpec(memory_space=pltpu.HBM)
    grid = pltpu.VMEM((chips, 128), I32)
    block = pltpu.VMEM((rows_dev, 128), F32)
    dma = pltpu.SemaphoreType.DMA
    return pl.pallas_call(
        round_kernel,
        in_specs=[hbm] * 4,
        out_specs=[vmem] * 8,
        out_shape=(
            jax.ShapeDtypeStruct((2, PLANE, NZ, 2, 128), I32),
            jax.ShapeDtypeStruct((K * 8, 128), F32),
            jax.ShapeDtypeStruct((nrow, 128), I32),
            jax.ShapeDtypeStruct((PITCH, 128), I32),
            jax.ShapeDtypeStruct((8, 128), F32),
            jax.ShapeDtypeStruct((READY * STEP, nrow * 128), BF16),
            jax.ShapeDtypeStruct((rows_dev, 128), I32),
            jax.ShapeDtypeStruct((READY, rows_dev, STEP), BF16),
        ),
        scratch_shapes=[
            pltpu.VMEM(candidates.shape, I32),
            pltpu.VMEM(candidates.shape, I32),
            pltpu.VMEM(current.shape, F32),
            pltpu.VMEM(candidates.shape, I32),
            pltpu.VMEM((2 * rows_dev, width), BF16),
            pltpu.VMEM((chips, CAP, width), BF16),
            pltpu.VMEM((chips, CAP, width), BF16),
            grid, grid, grid,
            pltpu.VMEM((2 * chips, 128), I32),
            grid,
            pltpu.VMEM((nrow, 128), I32),
            pltpu.VMEM((nrow, 128), I32),
            pltpu.VMEM((128, nrow), I32),
            pltpu.VMEM((nrow * 8, 128), F32),
            pltpu.VMEM((rows_dev, 128), I32),
            pltpu.VMEM((rows_dev, width), F32),
            pltpu.VMEM((256, width), BF16),
            block, block, block,
            pltpu.VMEM((K * 8, 128), F32),
            pltpu.VMEM((chips * 2, rows_dev), BF16),
            pltpu.VMEM((512, rows_dev), BF16),
            pltpu.VMEM((chips, 2, 128), I32),
            pltpu.VMEM((NZ, PLANE, 2, 128), I32),
            pltpu.VMEM((rows_dev // 128 * K, 128), F32),
            dma((4,)), dma, dma, dma((NZ,)), dma((NZ,)), dma((2 * PLANE,)), dma((2 * PLANE,)),
            dma, dma((NZ,)), dma, dma((NZ,)), dma((NZ,)), dma((2 * PLANE,)), dma((2 * PLANE,)),
        ],
        compiler_params=pltpu.CompilerParams(
            collective_id=0, has_side_effects=True, vmem_limit_bytes=34 << 20
        ),
        name="one_round",
    )(*[pltpu.with_memory_space_constraint(v, pltpu.HBM) for v in (candidates, flags, embeddings, current)])


def merge_kernel(
    back_ref, near_ref, pos_ref, row_ref, info_ref, q_ref, start_ref, hit_ref,
    out_ref, pay_ref, s_ref, x_ref, acc_ref, hot_ref,
):
    rows_dev = out_ref.shape[1]
    chips = back_ref.shape[1]
    lanes = iota((chips, 128), 1)
    group = lax.shift_right_logical(lanes, 5)
    first = (lanes & 16) == 0
    total = jnp.max(info_ref[0:1, :]).astype(I32)
    most = jnp.max(info_ref[1:2, :]).astype(I32)
    for h in range(2):
        for rr in range(2):
            words = back_ref[h, :, rr, :]
            low = (words & 65535).astype(F32)
            high = lax.shift_right_logical(words, 16).astype(F32)
            even = jnp.where(first, low, pltpu.roll(high, 16, 1))
            odd = jnp.where(first, pltpu.roll(low, 112, 1), high)
            for q in range(8):
                n = (h * CAP + rr * 8 + q) * chips
                hi, mid = split2(jnp.where(group == q // 2, odd if q & 1 else even, 0.0))
                pay_ref[n : n + chips, 0:128] = hi
                pay_ref[n : n + chips, 128:256] = mid
    steps = (total + STEP - 1) // STEP
    width = pay_ref.shape[0]

    def place_rows(t, hot):
        got = dot(hot, pay_ref[...], NN)
        for i in range(STEP // 128):
            at = slice(i * 128, (i + 1) * 128)
            turned = (got[at, 0:128] + got[at, 128:256]).T
            vals = turned[0:32] + turned[32:64] + turned[64:96] + turned[96:128]
            s_ref[pl.ds(t * (STEP // 128) + i, K, stride=PITCH), :] = vals

    def gather(t, carry):
        place_rows(t, q_ref[pl.ds(pl.multiple_of(t * STEP, STEP), STEP), :])
        return carry

    def gather_more(t, carry):
        place_rows(t, onehot(pos_ref[...] == t * STEP + iota((STEP, width), 0)))
        return carry

    lax.fori_loop(0, jnp.minimum(steps, READY), gather, 0)
    lax.fori_loop(READY, steps, gather_more, 0)
    lane = iota((8, 128), 1)
    groups = (total + 1023) // 1024

    def ahead(ref, at, s):
        here = ref[pl.ds(at, 8), :]
        after = ref[pl.ds(at + 1, 8), :]
        return after if s == 128 else pltpu.roll(jnp.where(lane >= s, here, after), 128 - s, 1)

    for e in range(8):

        @pl.when(most > 1 << e)
        def _():
            def step(g, carry):
                at = pl.multiple_of(g * 8, 8)
                same = row_ref[pl.ds(at, 8), :] == ahead(row_ref, at, 1 << e)
                mins = []
                for k in range(K):
                    later = ahead(s_ref, (K - 1 - k) * PITCH + at, 1 << e)
                    mins.append(jnp.minimum(s_ref[pl.ds(k * PITCH + at, 8), :], jnp.where(same, later, FAR)))
                best = merge_low(mins)
                for k in range(K):
                    s_ref[pl.ds(k * PITCH + at, 8), :] = best[k]
                return carry

            lax.fori_loop(0, groups, step, 0)

    acc_ref[...] = jnp.zeros_like(acc_ref)

    def expand_by(t, hot):
        cells = [s_ref[pl.ds(t * (STEP // 128) + i, K, stride=PITCH), :] for i in range(STEP // 128)]
        vals = jnp.concatenate(cells, axis=1)
        live = t * STEP + iota((K, STEP), 1) < total
        hi, mid = split2(jnp.where(live, vals, 0.0))
        ones = jnp.ones((K // 2, STEP), BF16)
        acc_ref[...] = acc_ref[...] + dot(jnp.concatenate([hi, mid, ones], axis=0), hot, NT)

    def expand(t, carry):
        expand_by(t, hit_ref[t])
        return carry

    def expand_more(t, carry):
        for i in range(STEP // 128):
            at = slice(i * 128, (i + 1) * 128)
            p = t * STEP + i * 128 + iota((rows_dev, 128), 1)
            hot_ref[:, at] = onehot(start_ref[...] == p)
        expand_by(t, hot_ref[...])
        return carry

    lax.fori_loop(0, jnp.minimum(steps, READY), expand, 0)
    lax.fori_loop(READY, steps, expand_more, 0)
    for b in range(rows_dev // 128):
        at = slice(b * 128, (b + 1) * 128)
        named = acc_ref[2 * K : 2 * K + 1, at] > 0.5
        x_ref[b * K : (b + 1) * K, :] = jnp.where(
            named, (acc_ref[0:K, at] + acc_ref[K : 2 * K, at]) * (1.0 / SCALE), FAR
        )
    have = near_ref[...]
    got = [x_ref[pl.ds(k, 8, stride=K), :] for k in range(K)]
    mins = [
        jnp.minimum(have[k * 8 : (k + 1) * 8, :], got[K - 1 - k])
        for k in range(K)
    ]
    best = merge_low(mins)
    for k in range(K):
        x_ref[k * 8 : (k + 1) * 8, :] = best[k]
    for b in range(rows_dev // 128):
        out_ref[:, b * 128 : (b + 1) * 128] = x_ref[pl.ds(b, K, stride=8), :]


def merge(back, best, pos, row, info, q, start, hit):
    rows_dev = start.shape[0]
    vmem = pl.BlockSpec(memory_space=pltpu.VMEM)
    return pl.pallas_call(
        merge_kernel,
        in_specs=[vmem] * 8,
        out_specs=vmem,
        out_shape=jax.ShapeDtypeStruct((K, rows_dev), F32),
        scratch_shapes=[
            pltpu.VMEM((pos.shape[1], 256), BF16),
            pltpu.VMEM((K * PITCH, 128), F32),
            pltpu.VMEM((rows_dev // 128 * K, 128), F32),
            pltpu.VMEM((2 * K + K // 2, rows_dev), F32),
            pltpu.VMEM((rows_dev, STEP), BF16),
        ],
        compiler_params=pltpu.CompilerParams(vmem_limit_bytes=20 << 20),
        name="merge",
    )(back, best, pos, row, info, q, start, hit)


def per_device(embeddings, candidates, fresh_flags, current):
    chips = lax.axis_size("rows")
    back, best, pos, row, info, q, start, hit = one_round(
        candidates, fresh_flags, embeddings, current.T, chips
    )
    back = back.reshape(2, chips, 2, 128)
    return merge(back, best, pos.reshape(1, -1), row, info, q, start, hit).T


def solution(mesh):
    spec = P(("rows", "sub"), None)
    return jax.shard_map(
        per_device, mesh=mesh, in_specs=(spec,) * 4, out_specs=spec, check_vma=False
    )
```

time: 130 us -> 121 us (0.931)
  local copies, waits for them, and re-layouts: 6.11 us -> 0 us
  Pallas kernels: 124 us -> 121 us
    unnamed x9 -> x0, local copies, waits for them, and re-layouts: 5.28 us -> none
    pallas_call x3 -> x2, Pallas kernels: 124 us -> 121 us  [the longest x1 114 us: one_round(): pl.pallas_call(round_kernel, in_specs=[hbm] * 4, out_specs=[vmem] * 8, ou...]
where the time goes in v3:
time: 121 us
  Pallas kernels  121 us (100%)
    pallas_call x1, Pallas kernels, one_round(): pl.pallas_call(round_kernel, in_specs=[hbm] * 4, out_specs=[vmem] * 8, ou...  114 us
    pallas_call x1, Pallas kernels, merge(): pl.pallas_call(merge_kernel, in_specs=[vmem] * 8, out_specs=vmem, out_sha...  6.86 us

profile of v3, /device:TPU:1, one launch (start us, length us, event | category | flops | bytes accessed | tf_op | source)
XLA Modules:
  0.0 120.7 jit_solution(6284024056340843254)
XLA Ops:
  0.0 113.9 %one_round.1 = (s32[2,16,8,2,128]{4,3,2,1,0:T(2,128)S(1)}, f32[256,128]{1,0:T(8,128)S(1)}, s32[32,128]{1,0:T(8,128)S(1)}, s32[40,128]{1,0:T(8,128)S(1)}, f32[8,1...) custom-call(s32[8,128]{1,0:T(8,128)} %cand_hbm.1, ...), custom_call_target="tpu_custom_call" | custom-call | tf_op jit(solution)/shard_map/one_round/pallas_call | solution.py:485
  113.9 6.9 %merge.1 = f32[32,1024]{1,0:T(8,128)} custom-call(s32[2,128,2,128]{3,2,1,0:T(2,128)S(1)} %bitcast.4, f32[256,128]{1,0:T(8,128)S(1)} %get-tuple-element.14.near_ref, s32[1,4096]{1,0:T(1,128)S(1)} %bitcast.5, s32[40,128]{1,0:T(8,128)S(1)} %get-tuple-element.16.row_ref, f32[8,128]{1,0:T(8,128)S(1)} %get-tuple-element.17.info_ref, ...), custom_call_target="tpu_custom_call" | custom-call | tf_op jit(solution)/shard_map/merge/pallas_call | solution.py:650

commit v4 on v3

--- a/solution.py
+++ b/solution.py
@@ -92,8 +92,12 @@
     return lax.div(chip, NZ * NX), lax.rem(lax.div(chip, NX), NZ), lax.rem(chip, NX), lax.axis_index("sub")
 
 
+def wrap(v, n):
+    return jnp.where(v >= n, v - n, v)
+
+
 def chip_at(y, z, x):
-    return (lax.rem(y, NY) * NZ + lax.rem(z, NZ)) * NX + lax.rem(x, NX)
+    return (wrap(y, NY) * NZ + wrap(z, NZ)) * NX + wrap(x, NX)
 
 
 def column_peers(here):
@@ -101,35 +105,35 @@
     return [(dz, {"rows": chip_at(y, z + dz, x), "sub": side}) for dz in AWAY[1:]]
 
 
-def plane_peers(here):
+def plane_peers(here, cores=2):
     y, z, x, side = here
     return [
-        (dy, dx, h, {"rows": chip_at(y + dy, z, x + dx), "sub": lax.rem(side + h, 2)})
+        (dy, dx, h, {"rows": chip_at(y + dy, z, x + dx), "sub": 1 - side if h else side})
         for dy in range(NY)
         for dx in range(NX)
-        for h in range(2)
+        for h in range(cores)
         if dy + dx + h > 0
     ]
 
 
 def greet(here):
+    y, z, x, side = here
     sem = pltpu.get_barrier_semaphore()
-    peers = [p[-1] for p in column_peers(here)] + [p[-1] for p in plane_peers(here)]
+    peers = [p[-1] for p in column_peers(here)] + [p[-1] for p in plane_peers(here, 1)]
+    peers.append({"rows": chip_at(y, z, x), "sub": 1 - side})
     for device in peers:
         pl.semaphore_signal(sem, inc=1, device_id=device, device_id_type=MESH)
     return lambda: pl.semaphore_wait(sem, len(peers))
+
+
+def drain(ref, sem):
+    pltpu.make_async_copy(ref, ref, sem).wait()
 
 
 def remote(src, dst, send, recv, device):
     return pltpu.make_async_remote_copy(
         src_ref=src, dst_ref=dst, send_sem=send, recv_sem=recv, device_id=device, device_id_type=MESH
     )
-
-
-def away(k):
-    m = k - 1
-    dz = jnp.where(lax.rem(m, 2) == 1, 4 - lax.div(m + 1, 2), 4 + lax.div(m, 2))
-    return jnp.where(k == 0, 0, dz)
 
 
 def far_rank(dz):
@@ -249,10 +253,10 @@
     cand_hbm, flag_hbm, emb_hbm, cur_hbm,
     back_ref, near_ref, pos_ref, row_ref, info_ref, q_ref, start_ref, hit_ref,
     c_ref, flag_ref, cur_ref, slot_ref,
-    rows_ref, served_ref, pulled_ref, w_ref, d_ref, e_ref, fin_ref, ask_ref,
+    rows_ref, served_ref, pulled_ref, w_ref, d_ref, e_ref, fin_ref,
     key_ref, lv_ref, col_ref, acc_ref, end_ref,
     cand_ref, z_ref, f_ref, a_ref, fwd_ref, t_ref, hot_ref, pay_ref, w2_ref, d2_ref, s_ref,
-    in_sem, half_send, half_recv, col_send, col_recv, plane_send, plane_recv,
+    in_sem, half_send, half_recv, col_send, col_recv, plane_send, plane_recv, tell_send, tell_recv,
     out_send, out_recv, own_sem, col_send2, col_recv2, plane_send2, plane_recv2,
 ):
     here = place()
@@ -275,73 +279,63 @@
     slots_of(c_ref, w_ref, slot_ref, span.bit_length() - 1)
     wait_for_peers()
 
-    copies = []
     for dz, device in column_peers(here):
-        src = w_ref.at[pl.ds(pl.multiple_of(lax.rem(z + dz, NZ) * PLANE, PLANE), PLANE)]
+        src = w_ref.at[pl.ds(pl.multiple_of(wrap(z + dz, NZ) * PLANE, PLANE), PLANE)]
         dst = d_ref.at[pl.ds(far_rank(-dz) * PLANE, PLANE)]
-        copies.append(remote(src, dst, col_send.at[dz], col_recv.at[dz], device))
-        copies[-1].start()
-    half = remote(emb_hbm, my_half, half_send, half_recv, {"rows": chip_at(y, z, x), "sub": 1 - side})
+        remote(src, dst, col_send, col_recv, device).start()
+    other = {"rows": chip_at(y, z, x), "sub": 1 - side}
+    half = remote(emb_hbm, my_half, half_send, half_recv, other)
     half.start()
     own = pl.ds(pl.multiple_of(z * PLANE, PLANE), PLANE)
     d_ref[far_rank(0) * PLANE : (far_rank(0) + 1) * PLANE, :] = w_ref[own, :]
-    for copy in copies:
-        copy.wait()
-    copies = []
-    for dy, dx, h, device in plane_peers(here):
+    column = pl.ds(0, (NZ - 1) * PLANE)
+    drain(d_ref.at[column], col_recv)
+    for dy, dx, _, device in plane_peers(here, 1):
         i = plane_rank(dy, dx)
-        if h == 0 or i == 0:
-            cell = lax.rem(y + dy, NY) * NX + lax.rem(x + dx, NX)
-            e_ref[i * NZ : (i + 1) * NZ, :] = d_ref[pl.ds(cell, NZ, stride=PLANE), :]
-        at = h * chips + plane_rank(-dy, -dx) * NZ
-        copies.append(
-            remote(
-                e_ref.at[pl.ds(i * NZ, NZ)], fin_ref.at[pl.ds(at, NZ)],
-                plane_send.at[2 * i + h], plane_recv.at[2 * i + h], device,
-            )
-        )
-        copies[-1].start()
-    fin_ref[0:NZ, :] = e_ref[0:NZ, :]
-    for copy in copies:
-        copy.wait()
-    for k in range(NZ):
-        ask_ref[k * PLANE : (k + 1) * PLANE, :] = fin_ref[pl.ds(k, PLANE, stride=NZ), :]
+        cell = wrap(y + dy, NY) * NX + wrap(x + dx, NX)
+        e_ref[i * NZ : (i + 1) * NZ, :] = d_ref[pl.ds(cell, NZ, stride=PLANE), :]
+        dst = fin_ref.at[pl.ds(plane_rank(-dy, -dx) * NZ, NZ)]
+        remote(e_ref.at[pl.ds(i * NZ, NZ)], dst, plane_send, plane_recv, device).start()
+    fin_ref[0:NZ, :] = d_ref[pl.ds(y * NX + x, NZ, stride=PLANE), :]
+    plane = pl.ds(0, (PLANE - 1) * NZ)
     for copy in brought[1:]:
         copy.wait()
     half.wait()
+    drain(fin_ref.at[plane], plane_recv)
+    tell = remote(fin_ref.at[pl.ds(0, chips)], fin_ref.at[pl.ds(chips, chips)], tell_send, tell_recv, other)
+    tell.start()
 
     spread = iota((128, 128), 1) == (iota((128, 128), 0) & (CAP - 1))
     ids = iota((128, span), 1)
-    me = z * PLANE + y * NX + x
-    part = PLANE // 2
-
-    def serve(t, carry):
-        asked = ask_ref[pl.ds(pl.multiple_of(t * part, part), part), :]
-        wide = jnp.concatenate([jnp.broadcast_to(asked[j : j + 1, :], (CAP, 128)) for j in range(part)], axis=0)
+    me = (y * NX + x) * NZ + z
+
+    def serve(c, carry):
+        asked = fin_ref[pl.ds(pl.multiple_of(c * NZ, NZ), NZ), :]
+        wide = jnp.concatenate([jnp.broadcast_to(asked[j : j + 1, :], (CAP, 128)) for j in range(NZ)], axis=0)
         col = jnp.sum(jnp.where(spread, wide, 0), axis=1, keepdims=True)
         got = dot(onehot(col == ids), rows_ref[...], NN).astype(BF16)
-        for j in range(part):
-            served_ref[t * part + j] = got[j * CAP : (j + 1) * CAP, :]
-        k = lax.div(t, 2)
-        dz = away(k)
+        for j in range(NZ):
+            served_ref[c * NZ + j] = got[j * CAP : (j + 1) * CAP, :]
+        y_to = wrap(y + lax.div(c, NX), NY)
+        x_to = wrap(x + lax.rem(c, NX), NX)
 
         def send(j):
-            i = lax.rem(t, 2) * part + j
-            device = {"rows": chip_at(y + lax.div(i, NX), z + dz, x + lax.rem(i, NX)), "sub": side}
-            remote(served_ref.at[t * part + j], pulled_ref.at[me], out_send, out_recv.at[k], device).start()
-
-        @pl.when(t > 0)
+            device = {"rows": (y_to * NZ + wrap(z + AWAY[j], NZ)) * NX + x_to, "sub": side}
+            remote(served_ref.at[c * NZ + j], pulled_ref.at[me], out_send, out_recv.at[c], device).start()
+
+        @pl.when(c > 0)
         def _():
             send(0)
 
-        for j in range(1, part):
+        for j in range(1, NZ):
             send(j)
         return carry
 
-    lax.fori_loop(0, 2 * NZ, serve, 0)
+    lax.fori_loop(0, PLANE, serve, 0)
     stay = pltpu.make_async_copy(served_ref.at[0], pulled_ref.at[me], own_sem)
     stay.start()
 
+    tell.wait()
     turned = [fin_ref[h * chips : (h + 1) * chips, :].T[0:CAP, :] for h in range(2)]
     plan_way_back(
         jnp.concatenate(turned, axis=0) - side * rows_dev,
@@ -360,39 +354,55 @@
             p = iota((rows_dev, 128), 1) + (t * STEP + i * 128)
             hit_ref[t, :, i * 128 : (i + 1) * 128] = onehot(start_ref[...] == p)
 
-    slot_cols = slot_ref[...].T
+    slots = slot_ref[...]
+    column_id = lax.shift_right_logical(slots, 4) & (PLANE - 1)
+    in_column = lax.shift_right_logical(slots, 8) * CAP + (slots & (CAP - 1))
+    column_cols = column_id.T
+    in_cols = in_column.T
     blocks = slot_ref.shape[0]
-    size = PLANE * CAP
-
-    def arrived(k, count):
-        got = pulled_ref.at[pl.ds(0, count)]
-        pltpu.make_async_copy(got, got, out_recv.at[k]).wait()
-        return lax.rem(z - away(k) + NZ, NZ)
-
-    def picked(b, plane, rows):
-        pick = onehot(slot_cols[:, b : b + 1] - plane * size == iota((128, size), 1))
-        return dot(pick, rows, NN)
-
-    def plane_rows(plane):
-        return pulled_ref[pl.ds(plane * PLANE, PLANE)].reshape(size, -1)
+    size = NZ * CAP
+    cells = iota((128, 2 * size), 1)
+
+    def source(c):
+        y_from = wrap(y + NY - lax.div(c, NX), NY)
+        return y_from * NX + wrap(x + NX - lax.rem(c, NX), NX)
+
+    def arrived(c, count):
+        drain(pulled_ref.at[pl.ds(0, count)], out_recv.at[c])
+
+    def column_rows(c):
+        return pulled_ref[pl.ds(source(c) * NZ, NZ)].reshape(size, -1)
+
+    def picked(b, c, rows):
+        here, there = source(c), source(c + 1)
+        col, at = column_cols[:, b : b + 1], in_cols[:, b : b + 1]
+        at = jnp.where(col == here, at, jnp.where(col == there, at + size, -1))
+        return dot(onehot(at == cells), rows, NN)
+
+    def two_columns(c):
+        return jnp.concatenate([column_rows(c), column_rows(c + 1)], axis=0)
 
     stay.wait()
-    plane = arrived(0, PLANE - 1)
-    rows = plane_rows(plane)
+    arrived(0, NZ - 1)
+    arrived(1, NZ)
+    rows = two_columns(0)
     for b in range(blocks):
-        cand_ref[b * 128 : (b + 1) * 128, :] = picked(b, plane, rows)
+        cand_ref[b * 128 : (b + 1) * 128, :] = picked(b, 0, rows)
 
     def more_rows(k, carry):
-        plane = arrived(k, PLANE)
-        rows = plane_rows(plane)
+        arrived(2 * k, NZ)
+        arrived(2 * k + 1, NZ)
+        rows = two_columns(2 * k)
         for b in range(blocks):
             at = slice(b * 128, (b + 1) * 128)
-            cand_ref[at, :] = cand_ref[at, :] + picked(b, plane, rows)
-        return carry
-
-    lax.fori_loop(1, NZ - 1, more_rows, 0)
-    plane = arrived(NZ - 1, PLANE)
-    rows = plane_rows(plane)
+            cand_ref[at, :] = cand_ref[at, :] + picked(b, 2 * k, rows)
+        return carry
+
+    lax.fori_loop(1, PLANE // 2 - 1, more_rows, 0)
+    last = PLANE - 2
+    arrived(last, NZ)
+    arrived(last + 1, NZ)
+    rows = two_columns(last)
 
     flags = flag_ref[...]
     flag_cols = flags.T
@@ -401,7 +411,7 @@
     for b in range(blocks):
         at = slice(b * 128, (b + 1) * 128)
         z_ref[0:128, :] = rows_ref[pl.ds(half_at + b * 128, 128), :]
-        z_ref[128:256, :] = (cand_ref[at, :] + picked(b, plane, rows)).astype(BF16)
+        z_ref[128:256, :] = (cand_ref[at, :] + picked(b, last, rows)).astype(BF16)
         both = z_ref[...]
         gram = dot(both, both, NT)
         diag = jnp.where(eye, gram, 0.0)
@@ -447,31 +457,29 @@
     words = low + lax.shift_left(high, 16)
     for n in range(chips):
         w2_ref[n] = words[2 * n : 2 * n + 2, :]
-    copies = []
     for dz, device in column_peers(here):
-        src = w2_ref.at[pl.ds(lax.rem(z + dz, NZ) * PLANE, PLANE)]
-        copies.append(remote(src, d2_ref.at[far_rank(-dz)], col_send2.at[dz], col_recv2.at[dz], device))
-        copies[-1].start()
+        src = w2_ref.at[pl.ds(wrap(z + dz, NZ) * PLANE, PLANE)]
+        remote(src, d2_ref.at[far_rank(-dz)], col_send2, col_recv2, device).start()
     stay = pltpu.make_async_copy(w2_ref.at[pl.ds(z * PLANE, PLANE)], d2_ref.at[far_rank(0)], own_sem)
     stay.start()
     near(fwd_ref, cur_ref, near_ref, s_ref)
     stay.wait()
-    for copy in copies:
-        copy.wait()
-    copies = []
+    drain(d2_ref.at[pl.ds(1, NZ - 1)], col_recv2)
     for dy, dx, h, device in plane_peers(here):
-        i = plane_rank(dy, dx)
-        cell = lax.rem(y + dy, NY) * NX + lax.rem(x + dx, NX)
+        cell = wrap(y + dy, NY) * NX + wrap(x + dx, NX)
         dst = back_ref.at[h, plane_rank(-dy, -dx)]
-        copies.append(remote(d2_ref.at[:, cell], dst, plane_send2.at[2 * i + h], plane_recv2.at[2 * i + h], device))
-        copies[-1].start()
+        remote(d2_ref.at[:, cell], dst, plane_send2.at[h], plane_recv2.at[h], device).start()
     stay = pltpu.make_async_copy(d2_ref.at[:, y * NX + x], back_ref.at[0, 0], own_sem)
     stay.start()
+    drain(d_ref.at[column], col_send)
+    drain(fin_ref.at[plane], plane_send)
+    drain(served_ref.at[pl.ds(0, chips - 1)], out_send)
+    drain(d2_ref.at[pl.ds(1, NZ - 1)], col_send2)
     stay.wait()
-    for copy in copies:
-        copy.wait()
-    sent = served_ref.at[pl.ds(0, chips - 1)]
-    pltpu.make_async_copy(sent, sent, out_send).wait()
+    drain(back_ref.at[0, pl.ds(1, PLANE - 1)], plane_recv2.at[0])
+    drain(back_ref.at[1], plane_recv2.at[1])
+    drain(back_ref.at[0, pl.ds(1, PLANE - 1)], plane_send2.at[0])
+    drain(back_ref.at[1], plane_send2.at[1])
 
 
 def one_round(candidates, flags, embeddings, current, chips):
@@ -506,7 +514,6 @@
             pltpu.VMEM((chips, CAP, width), BF16),
             grid, grid, grid,
             pltpu.VMEM((2 * chips, 128), I32),
-            grid,
             pltpu.VMEM((nrow, 128), I32),
             pltpu.VMEM((nrow, 128), I32),
             pltpu.VMEM((128, nrow), I32),
@@ -521,8 +528,8 @@
             pltpu.VMEM((chips, 2, 128), I32),
             pltpu.VMEM((NZ, PLANE, 2, 128), I32),
             pltpu.VMEM((rows_dev // 128 * K, 128), F32),
-            dma((4,)), dma, dma, dma((NZ,)), dma((NZ,)), dma((2 * PLANE,)), dma((2 * PLANE,)),
-            dma, dma((NZ,)), dma, dma((NZ,)), dma((NZ,)), dma((2 * PLANE,)), dma((2 * PLANE,)),
+            dma((4,)), dma, dma, dma, dma, dma, dma, dma, dma,
+            dma, dma((PLANE,)), dma, dma, dma, dma((2,)), dma((2,)),
         ],
         compiler_params=pltpu.CompilerParams(
             collective_id=0, has_side_effects=True, vmem_limit_bytes=34 << 20

time: 121 us -> 111 us (0.917)
  Pallas kernels: 121 us -> 111 us
    pallas_call x1, Pallas kernels: 114 us -> 105 us  [one_round(): pl.pallas_call(round_kernel, in_specs=[hbm] * 4, out_specs=[vmem] * 8, ou...]
where the time goes in v4:
time: 111 us
  Pallas kernels  111 us (100%)
    pallas_call x1, Pallas kernels, one_round(): pl.pallas_call(round_kernel, in_specs=[hbm] * 4, out_specs=[vmem] * 8, ou...  105 us
    pallas_call x1, Pallas kernels, merge(): pl.pallas_call(merge_kernel, in_specs=[vmem] * 8, out_specs=vmem, out_sha...  6.49 us

profile of v4, /device:TPU:1, one launch (start us, length us, event | category | flops | bytes accessed | tf_op | source)
XLA Modules:
  0.0 111.4 jit_solution(75070527511158648)
XLA Ops:
  0.0 104.9 %one_round.1 = (s32[2,16,8,2,128]{4,3,2,1,0:T(2,128)S(1)}, f32[256,128]{1,0:T(8,128)S(1)}, s32[32,128]{1,0:T(8,128)S(1)}, s32[40,128]{1,0:T(8,128)S(1)}, f32[8,1...) custom-call(s32[8,128]{1,0:T(8,128)} %cand_hbm.1, ...), custom_call_target="tpu_custom_call" | custom-call | tf_op jit(solution)/shard_map/one_round/pallas_call | solution.py:493
  104.9 6.5 %merge.1 = f32[32,1024]{1,0:T(8,128)} custom-call(s32[2,128,2,128]{3,2,1,0:T(2,128)S(1)} %bitcast.4, f32[256,128]{1,0:T(8,128)S(1)} %get-tuple-element.14.near_ref, s32[1,4096]{1,0:T(1,128)S(1)} %bitcast.5, s32[40,128]{1,0:T(8,128)S(1)} %get-tuple-element.16.row_ref, f32[8,128]{1,0:T(8,128)S(1)} %get-tuple-element.17.info_ref, ...), custom_call_target="tpu_custom_call" | custom-call | tf_op jit(solution)/shard_map/merge/pallas_call | solution.py:657

commit v5 on v4

--- a/solution.py
+++ b/solution.py
@@ -278,14 +278,14 @@
     brought[0].wait()
     slots_of(c_ref, w_ref, slot_ref, span.bit_length() - 1)
     wait_for_peers()
+    other = {"rows": chip_at(y, z, x), "sub": 1 - side}
+    half = remote(emb_hbm, my_half, half_send, half_recv, other)
+    half.start()
 
     for dz, device in column_peers(here):
         src = w_ref.at[pl.ds(pl.multiple_of(wrap(z + dz, NZ) * PLANE, PLANE), PLANE)]
         dst = d_ref.at[pl.ds(far_rank(-dz) * PLANE, PLANE)]
         remote(src, dst, col_send, col_recv, device).start()
-    other = {"rows": chip_at(y, z, x), "sub": 1 - side}
-    half = remote(emb_hbm, my_half, half_send, half_recv, other)
-    half.start()
     own = pl.ds(pl.multiple_of(z * PLANE, PLANE), PLANE)
     d_ref[far_rank(0) * PLANE : (far_rank(0) + 1) * PLANE, :] = w_ref[own, :]
     column = pl.ds(0, (NZ - 1) * PLANE)
@@ -301,37 +301,39 @@
     for copy in brought[1:]:
         copy.wait()
     half.wait()
-    drain(fin_ref.at[plane], plane_recv)
-    tell = remote(fin_ref.at[pl.ds(0, chips)], fin_ref.at[pl.ds(chips, chips)], tell_send, tell_recv, other)
-    tell.start()
 
     spread = iota((128, 128), 1) == (iota((128, 128), 0) & (CAP - 1))
     ids = iota((128, span), 1)
     me = (y * NX + x) * NZ + z
 
     def serve(c, carry):
-        asked = fin_ref[pl.ds(pl.multiple_of(c * NZ, NZ), NZ), :]
+        asked = fin_ref[0:NZ, :] if isinstance(c, int) else fin_ref[pl.ds(pl.multiple_of(c * NZ, NZ), NZ), :]
         wide = jnp.concatenate([jnp.broadcast_to(asked[j : j + 1, :], (CAP, 128)) for j in range(NZ)], axis=0)
         col = jnp.sum(jnp.where(spread, wide, 0), axis=1, keepdims=True)
         got = dot(onehot(col == ids), rows_ref[...], NN).astype(BF16)
         for j in range(NZ):
             served_ref[c * NZ + j] = got[j * CAP : (j + 1) * CAP, :]
-        y_to = wrap(y + lax.div(c, NX), NY)
-        x_to = wrap(x + lax.rem(c, NX), NX)
+        y_to = wrap(y + c // NX, NY)
+        x_to = wrap(x + c % NX, NX)
 
         def send(j):
             device = {"rows": (y_to * NZ + wrap(z + AWAY[j], NZ)) * NX + x_to, "sub": side}
             remote(served_ref.at[c * NZ + j], pulled_ref.at[me], out_send, out_recv.at[c], device).start()
 
-        @pl.when(c > 0)
-        def _():
+        if isinstance(c, int):
+            assert c == 0
+        else:
             send(0)
-
         for j in range(1, NZ):
             send(j)
         return carry
 
-    lax.fori_loop(0, PLANE, serve, 0)
+    serve(0, 0)
+    drain(fin_ref.at[plane], plane_recv)
+    tell = remote(fin_ref.at[pl.ds(0, chips)], fin_ref.at[pl.ds(chips, chips)], tell_send, tell_recv, other)
+    tell.start()
+
+    lax.fori_loop(1, PLANE, serve, 0)
     stay = pltpu.make_async_copy(served_ref.at[0], pulled_ref.at[me], own_sem)
     stay.start()
 
@@ -349,10 +351,8 @@
         return carry
 
     lax.fori_loop(0, READY * STEP // 128, ready, 0)
-    for t in range(READY):
-        for i in range(STEP // 128):
-            p = iota((rows_dev, 128), 1) + (t * STEP + i * 128)
-            hit_ref[t, :, i * 128 : (i + 1) * 128] = onehot(start_ref[...] == p)
+    for i in range(READY * STEP // 128):
+        hit_ref[:, i * 128 : (i + 1) * 128] = onehot(start_ref[...] == iota((rows_dev, 128), 1) + i * 128)
 
     slots = slot_ref[...]
     column_id = lax.shift_right_logical(slots, 4) & (PLANE - 1)
@@ -502,7 +502,7 @@
             jax.ShapeDtypeStruct((8, 128), F32),
             jax.ShapeDtypeStruct((READY * STEP, nrow * 128), BF16),
             jax.ShapeDtypeStruct((rows_dev, 128), I32),
-            jax.ShapeDtypeStruct((READY, rows_dev, STEP), BF16),
+            jax.ShapeDtypeStruct((rows_dev, READY * STEP), BF16),
         ),
         scratch_shapes=[
             pltpu.VMEM(candidates.shape, I32),
@@ -547,6 +547,7 @@
     lanes = iota((chips, 128), 1)
     group = lax.shift_right_logical(lanes, 5)
     first = (lanes & 16) == 0
+    keep = [onehot(group == u) for u in range(4)]
     total = jnp.max(info_ref[0:1, :]).astype(I32)
     most = jnp.max(info_ref[1:2, :]).astype(I32)
     for h in range(2):
@@ -556,31 +557,28 @@
             high = lax.shift_right_logical(words, 16).astype(F32)
             even = jnp.where(first, low, pltpu.roll(high, 16, 1))
             odd = jnp.where(first, pltpu.roll(low, 112, 1), high)
+            pieces = [split2(even), split2(odd)]
             for q in range(8):
                 n = (h * CAP + rr * 8 + q) * chips
-                hi, mid = split2(jnp.where(group == q // 2, odd if q & 1 else even, 0.0))
-                pay_ref[n : n + chips, 0:128] = hi
-                pay_ref[n : n + chips, 128:256] = mid
+                hi, mid = pieces[q & 1]
+                pay_ref[n : n + chips, 0:128] = hi * keep[q // 2]
+                pay_ref[n : n + chips, 128:256] = mid * keep[q // 2]
     steps = (total + STEP - 1) // STEP
     width = pay_ref.shape[0]
 
-    def place_rows(t, hot):
-        got = dot(hot, pay_ref[...], NN)
-        for i in range(STEP // 128):
+    def place_rows(base, got):
+        for i in range(got.shape[0] // 128):
             at = slice(i * 128, (i + 1) * 128)
             turned = (got[at, 0:128] + got[at, 128:256]).T
             vals = turned[0:32] + turned[32:64] + turned[64:96] + turned[96:128]
-            s_ref[pl.ds(t * (STEP // 128) + i, K, stride=PITCH), :] = vals
-
-    def gather(t, carry):
-        place_rows(t, q_ref[pl.ds(pl.multiple_of(t * STEP, STEP), STEP), :])
+            s_ref[pl.ds(base + i, K, stride=PITCH), :] = vals
+
+    def gather_more(t, carry):
+        hot = onehot(pos_ref[...] == t * STEP + iota((STEP, width), 0))
+        place_rows(t * (STEP // 128), dot(hot, pay_ref[...], NN))
         return carry
 
-    def gather_more(t, carry):
-        place_rows(t, onehot(pos_ref[...] == t * STEP + iota((STEP, width), 0)))
-        return carry
-
-    lax.fori_loop(0, jnp.minimum(steps, READY), gather, 0)
+    place_rows(0, dot(q_ref[...], pay_ref[...], NN))
     lax.fori_loop(READY, steps, gather_more, 0)
     lane = iota((8, 128), 1)
     groups = (total + 1023) // 1024
@@ -608,29 +606,22 @@
 
             lax.fori_loop(0, groups, step, 0)
 
-    acc_ref[...] = jnp.zeros_like(acc_ref)
-
-    def expand_by(t, hot):
-        cells = [s_ref[pl.ds(t * (STEP // 128) + i, K, stride=PITCH), :] for i in range(STEP // 128)]
-        vals = jnp.concatenate(cells, axis=1)
-        live = t * STEP + iota((K, STEP), 1) < total
+    def listed(base, n):
+        vals = jnp.concatenate([s_ref[pl.ds(base + i, K, stride=PITCH), :] for i in range(n)], axis=1)
+        live = base * 128 + iota((K, n * 128), 1) < total
         hi, mid = split2(jnp.where(live, vals, 0.0))
-        ones = jnp.ones((K // 2, STEP), BF16)
-        acc_ref[...] = acc_ref[...] + dot(jnp.concatenate([hi, mid, ones], axis=0), hot, NT)
-
-    def expand(t, carry):
-        expand_by(t, hit_ref[t])
-        return carry
+        return jnp.concatenate([hi, mid, jnp.ones((K // 2, n * 128), BF16)], axis=0)
+
+    acc_ref[...] = dot(listed(0, READY * STEP // 128), hit_ref[...], NT)
 
     def expand_more(t, carry):
         for i in range(STEP // 128):
             at = slice(i * 128, (i + 1) * 128)
             p = t * STEP + i * 128 + iota((rows_dev, 128), 1)
             hot_ref[:, at] = onehot(start_ref[...] == p)
-        expand_by(t, hot_ref[...])
+        acc_ref[...] = acc_ref[...] + dot(listed(t * (STEP // 128), STEP // 128), hot_ref[...], NT)
         return carry
 
-    lax.fori_loop(0, jnp.minimum(steps, READY), expand, 0)
     lax.fori_loop(READY, steps, expand_more, 0)
     for b in range(rows_dev // 128):
         at = slice(b * 128, (b + 1) * 128)

time: 111 us -> 107 us (0.964)
  Pallas kernels: 111 us -> 107 us
    pallas_call x1, Pallas kernels: 105 us -> 101 us  [one_round(): pl.pallas_call(round_kernel, in_specs=[hbm] * 4, out_specs=[vmem] * 8, ou...]
where the time goes in v5:
time: 107 us
  Pallas kernels  107 us (100%)
    pallas_call x1, Pallas kernels, one_round(): pl.pallas_call(round_kernel, in_specs=[hbm] * 4, out_specs=[vmem] * 8, ou...  101 us
    pallas_call x1, Pallas kernels, merge(): pl.pallas_call(merge_kernel, in_specs=[vmem] * 8, out_specs=vmem, out_sha...  5.85 us

profile of v5, /device:TPU:1, one launch (start us, length us, event | category | flops | bytes accessed | tf_op | source)
XLA Modules:
  0.0 107.0 jit_solution(10956336098546713104)
XLA Ops:
  0.0 101.2 %one_round.1 = (s32[2,16,8,2,128]{4,3,2,1,0:T(2,128)S(1)}, f32[256,128]{1,0:T(8,128)S(1)}, s32[32,128]{1,0:T(8,128)S(1)}, s32[40,128]{1,0:T(8,128)S(1)}, f32[8,1...) custom-call(s32[8,128]{1,0:T(8,128)} %cand_hbm.1, ...), custom_call_target="tpu_custom_call" | custom-call | tf_op jit(solution)/shard_map/one_round/pallas_call | solution.py:493
  101.2 5.8 %merge.1 = f32[32,1024]{1,0:T(8,128)} custom-call(s32[2,128,2,128]{3,2,1,0:T(2,128)S(1)} %bitcast.4, f32[256,128]{1,0:T(8,128)S(1)} %get-tuple-element.14.near_ref, s32[1,4096]{1,0:T(1,128)S(1)} %bitcast.5, s32[40,128]{1,0:T(8,128)S(1)} %get-tuple-element.16.row_ref, f32[8,128]{1,0:T(8,128)S(1)} %get-tuple-element.17.info_ref, ...), custom_call_target="tpu_custom_call" | custom-call | tf_op jit(solution)/shard_map/merge/pallas_call | solution.py:648

commit v6 on v5

--- a/solution.py
+++ b/solution.py
@@ -249,9 +249,13 @@
         out_ref[k * 8 : (k + 1) * 8, :] = best[k]
 
 
+def slot_row(n, u):
+    return n // 4 * CAP + n // 2 % 2 * 8 + 2 * u + n % 2
+
+
 def round_kernel(
     cand_hbm, flag_hbm, emb_hbm, cur_hbm,
-    back_ref, near_ref, pos_ref, row_ref, info_ref, q_ref, start_ref, hit_ref,
+    back_ref, near_ref, pos_ref, row_ref, info_ref, q_ref, start_ref, hit_ref, quad_ref,
     c_ref, flag_ref, cur_ref, slot_ref,
     rows_ref, served_ref, pulled_ref, w_ref, d_ref, e_ref, fin_ref,
     key_ref, lv_ref, col_ref, acc_ref, end_ref,
@@ -346,8 +350,17 @@
 
     def ready(t, carry):
         p = iota((128, 128), 0) + t * 128
-        for e in range(pos_ref.shape[0]):
-            q_ref[pl.ds(pl.multiple_of(t * 128, 128), 128), e * 128 : (e + 1) * 128] = onehot(pos_ref[e : e + 1, :] == p)
+        at = pl.ds(pl.multiple_of(t * 128, 128), 128)
+        quad = jnp.zeros((128, 128), F32)
+        for n in range(8):
+            found = jnp.zeros((128, 128), F32)
+            for u in range(4):
+                e = slot_row(n, u)
+                hit = jnp.where(pos_ref[e : e + 1, :] == p, 1.0, 0.0)
+                found = found + hit
+                quad = quad + hit * float(u)
+            q_ref[at, n * 128 : (n + 1) * 128] = found.astype(BF16)
+        quad_ref[pl.ds(t, 1), :] = jnp.sum(quad.T, axis=0, keepdims=True)
         return carry
 
     lax.fori_loop(0, READY * STEP // 128, ready, 0)
@@ -493,16 +506,17 @@
     return pl.pallas_call(
         round_kernel,
         in_specs=[hbm] * 4,
-        out_specs=[vmem] * 8,
+        out_specs=[vmem] * 9,
         out_shape=(
             jax.ShapeDtypeStruct((2, PLANE, NZ, 2, 128), I32),
             jax.ShapeDtypeStruct((K * 8, 128), F32),
             jax.ShapeDtypeStruct((nrow, 128), I32),
             jax.ShapeDtypeStruct((PITCH, 128), I32),
             jax.ShapeDtypeStruct((8, 128), F32),
-            jax.ShapeDtypeStruct((READY * STEP, nrow * 128), BF16),
+            jax.ShapeDtypeStruct((READY * STEP, nrow * 32), BF16),
             jax.ShapeDtypeStruct((rows_dev, 128), I32),
             jax.ShapeDtypeStruct((rows_dev, READY * STEP), BF16),
+            jax.ShapeDtypeStruct((16, 128), F32),
         ),
         scratch_shapes=[
             pltpu.VMEM(candidates.shape, I32),
@@ -539,15 +553,13 @@
 
 
 def merge_kernel(
-    back_ref, near_ref, pos_ref, row_ref, info_ref, q_ref, start_ref, hit_ref,
+    back_ref, near_ref, pos_ref, row_ref, info_ref, q_ref, start_ref, hit_ref, quad_ref,
     out_ref, pay_ref, s_ref, x_ref, acc_ref, hot_ref,
 ):
     rows_dev = out_ref.shape[1]
     chips = back_ref.shape[1]
     lanes = iota((chips, 128), 1)
-    group = lax.shift_right_logical(lanes, 5)
     first = (lanes & 16) == 0
-    keep = [onehot(group == u) for u in range(4)]
     total = jnp.max(info_ref[0:1, :]).astype(I32)
     most = jnp.max(info_ref[1:2, :]).astype(I32)
     for h in range(2):
@@ -557,28 +569,37 @@
             high = lax.shift_right_logical(words, 16).astype(F32)
             even = jnp.where(first, low, pltpu.roll(high, 16, 1))
             odd = jnp.where(first, pltpu.roll(low, 112, 1), high)
-            pieces = [split2(even), split2(odd)]
-            for q in range(8):
-                n = (h * CAP + rr * 8 + q) * chips
-                hi, mid = pieces[q & 1]
-                pay_ref[n : n + chips, 0:128] = hi * keep[q // 2]
-                pay_ref[n : n + chips, 128:256] = mid * keep[q // 2]
+            for parity, codes in enumerate((even, odd)):
+                n = (h * 4 + rr * 2 + parity) * chips
+                hi, mid = split2(codes)
+                pay_ref[n : n + chips, 0:128] = hi
+                pay_ref[n : n + chips, 128:256] = mid
     steps = (total + STEP - 1) // STEP
-    width = pay_ref.shape[0]
-
-    def place_rows(base, got):
-        for i in range(got.shape[0] // 128):
+
+    def place_rows(at, turned, quad):
+        parts = [turned[u * K : (u + 1) * K] for u in range(4)]
+        if quad is not None:
+            parts = [jnp.where(quad == float(u), part, 0.0) for u, part in enumerate(parts)]
+        s_ref[pl.ds(at, K, stride=PITCH), :] = parts[0] + parts[1] + parts[2] + parts[3]
+
+    def gather_more(t, carry):
+        p = t * STEP + iota((STEP, 128), 0)
+        quarter = lax.shift_right_logical(iota(pay_ref.shape, 1) & 127, 5)
+        got = jnp.zeros((STEP, 256), F32)
+        for u in range(4):
+            rows = [slot_row(n, u) * 128 for n in range(8)]
+            hot = jnp.concatenate([onehot(pos_ref[:, e : e + 128] == p) for e in rows], axis=1)
+            pay = jnp.where(quarter == u, pay_ref[...].astype(F32), 0.0).astype(BF16)
+            got = got + dot(hot, pay, NN)
+        for i in range(STEP // 128):
             at = slice(i * 128, (i + 1) * 128)
-            turned = (got[at, 0:128] + got[at, 128:256]).T
-            vals = turned[0:32] + turned[32:64] + turned[64:96] + turned[96:128]
-            s_ref[pl.ds(base + i, K, stride=PITCH), :] = vals
-
-    def gather_more(t, carry):
-        hot = onehot(pos_ref[...] == t * STEP + iota((STEP, width), 0))
-        place_rows(t * (STEP // 128), dot(hot, pay_ref[...], NN))
+            place_rows(t * (STEP // 128) + i, (got[at, 0:128] + got[at, 128:256]).T, None)
         return carry
 
-    place_rows(0, dot(q_ref[...], pay_ref[...], NN))
+    got = dot(q_ref[...], pay_ref[...], NN)
+    for i in range(READY * STEP // 128):
+        at = slice(i * 128, (i + 1) * 128)
+        place_rows(i, (got[at, 0:128] + got[at, 128:256]).T, quad_ref[i : i + 1, :])
     lax.fori_loop(READY, steps, gather_more, 0)
     lane = iota((8, 128), 1)
     groups = (total + 1023) // 1024
@@ -642,16 +663,16 @@
         out_ref[:, b * 128 : (b + 1) * 128] = x_ref[pl.ds(b, K, stride=8), :]
 
 
-def merge(back, best, pos, row, info, q, start, hit):
+def merge(back, best, pos, row, info, q, start, hit, quad):
     rows_dev = start.shape[0]
     vmem = pl.BlockSpec(memory_space=pltpu.VMEM)
     return pl.pallas_call(
         merge_kernel,
-        in_specs=[vmem] * 8,
+        in_specs=[vmem] * 9,
         out_specs=vmem,
         out_shape=jax.ShapeDtypeStruct((K, rows_dev), F32),
         scratch_shapes=[
-            pltpu.VMEM((pos.shape[1], 256), BF16),
+            pltpu.VMEM((pos.shape[1] // 4, 256), BF16),
             pltpu.VMEM((K * PITCH, 128), F32),
             pltpu.VMEM((rows_dev // 128 * K, 128), F32),
             pltpu.VMEM((2 * K + K // 2, rows_dev), F32),
@@ -659,16 +680,16 @@
         ],
         compiler_params=pltpu.CompilerParams(vmem_limit_bytes=20 << 20),
         name="merge",
-    )(back, best, pos, row, info, q, start, hit)
+    )(back, best, pos, row, info, q, start, hit, quad)
 
 
 def per_device(embeddings, candidates, fresh_flags, current):
     chips = lax.axis_size("rows")
-    back, best, pos, row, info, q, start, hit = one_round(
+    back, best, pos, row, info, q, start, hit, quad = one_round(
         candidates, fresh_flags, embeddings, current.T, chips
     )
     back = back.reshape(2, chips, 2, 128)
-    return merge(back, best, pos.reshape(1, -1), row, info, q, start, hit).T
+    return merge(back, best, pos.reshape(1, -1), row, info, q, start, hit, quad).T
 
 
 def solution(mesh):

time: 107 us -> 105 us (0.981)
  Pallas kernels: 107 us -> 105 us
    pallas_call x2, Pallas kernels: 107 us -> 105 us  [the longest x1 101 us: one_round(): pl.pallas_call(round_kernel, in_specs=[hbm] * 4, out_specs=[vmem] * 9, ou...]
where the time goes in v6:
time: 105 us
  Pallas kernels  105 us (100%)
    pallas_call x1, Pallas kernels, one_round(): pl.pallas_call(round_kernel, in_specs=[hbm] * 4, out_specs=[vmem] * 9, ou...  101 us
    pallas_call x1, Pallas kernels, merge(): pl.pallas_call(merge_kernel, in_specs=[vmem] * 9, out_specs=vmem, out_sha...  3.8 us

profile of v6, /device:TPU:1, one launch (start us, length us, event | category | flops | bytes accessed | tf_op | source)
XLA Modules:
  0.0 105.0 jit_solution(11600277392062364785)
XLA Ops:
  0.0 101.2 %one_round.1 = (s32[2,16,8,2,128]{4,3,2,1,0:T(2,128)S(1)}, f32[256,128]{1,0:T(8,128)S(1)}, s32[32,128]{1,0:T(8,128)S(1)}, s32[40,128]{1,0:T(8,128)S(1)}, f32[8,1...) custom-call(s32[8,128]{1,0:T(8,128)} %cand_hbm.1, ...), custom_call_target="tpu_custom_call" | custom-call | tf_op jit(solution)/shard_map/one_round/pallas_call | solution.py:506
  101.2 3.8 %merge.1 = f32[32,1024]{1,0:T(8,128)} custom-call(s32[2,128,2,128]{3,2,1,0:T(2,128)S(1)} %bitcast.4, f32[256,128]{1,0:T(8,128)S(1)} %get-tuple-element.15.near_ref, s32[1,4096]{1,0:T(1,128)S(1)} %bitcast.5, s32[40,128]{1,0:T(8,128)S(1)} %get-tuple-element.17.row_ref, f32[8,128]{1,0:T(8,128)S(1)} %get-tuple-element.18.info_ref, ...), custom_call_target="tpu_custom_call" | custom-call | tf_op jit(solution)/shard_map/merge/pallas_call | solution.py:669

commit v7 on v6

--- a/solution.py
+++ b/solution.py
@@ -259,7 +259,7 @@
     c_ref, flag_ref, cur_ref, slot_ref,
     rows_ref, served_ref, pulled_ref, w_ref, d_ref, e_ref, fin_ref,
     key_ref, lv_ref, col_ref, acc_ref, end_ref,
-    cand_ref, z_ref, f_ref, a_ref, fwd_ref, t_ref, hot_ref, pay_ref, w2_ref, d2_ref, s_ref,
+    cand_ref, z_ref, f_ref, a_ref, fwd_ref, t_ref, hot_ref, pay_ref, w2_ref, d2_ref, e2_ref, s_ref,
     in_sem, half_send, half_recv, col_send, col_recv, plane_send, plane_recv, tell_send, tell_recv,
     out_send, out_recv, own_sem, col_send2, col_recv2, plane_send2, plane_recv2,
 ):
@@ -478,11 +478,13 @@
     near(fwd_ref, cur_ref, near_ref, s_ref)
     stay.wait()
     drain(d2_ref.at[pl.ds(1, NZ - 1)], col_recv2)
+    for k in range(NZ):
+        e2_ref[:, k] = d2_ref[k]
     for dy, dx, h, device in plane_peers(here):
         cell = wrap(y + dy, NY) * NX + wrap(x + dx, NX)
         dst = back_ref.at[h, plane_rank(-dy, -dx)]
-        remote(d2_ref.at[:, cell], dst, plane_send2.at[h], plane_recv2.at[h], device).start()
-    stay = pltpu.make_async_copy(d2_ref.at[:, y * NX + x], back_ref.at[0, 0], own_sem)
+        remote(e2_ref.at[cell], dst, plane_send2.at[h], plane_recv2.at[h], device).start()
+    stay = pltpu.make_async_copy(e2_ref.at[y * NX + x], back_ref.at[0, 0], own_sem)
     stay.start()
     drain(d_ref.at[column], col_send)
     drain(fin_ref.at[plane], plane_send)
@@ -541,6 +543,7 @@
             pltpu.VMEM((512, rows_dev), BF16),
             pltpu.VMEM((chips, 2, 128), I32),
             pltpu.VMEM((NZ, PLANE, 2, 128), I32),
+            pltpu.VMEM((PLANE, NZ, 2, 128), I32),
             pltpu.VMEM((rows_dev // 128 * K, 128), F32),
             dma((4,)), dma, dma, dma, dma, dma, dma, dma, dma,
             dma, dma((PLANE,)), dma, dma, dma, dma((2,)), dma((2,)),

time: 105 us -> 105 us (level)
  no operation moved by 1% of the time
where the time goes in v7:
time: 105 us
  Pallas kernels  105 us (100%)
    pallas_call x1, Pallas kernels, one_round(): pl.pallas_call(round_kernel, in_specs=[hbm] * 4, out_specs=[vmem] * 9, ou...  101 us
    pallas_call x1, Pallas kernels, merge(): pl.pallas_call(merge_kernel, in_specs=[vmem] * 9, out_specs=vmem, out_sha...  3.8 us

profile of v7, /device:TPU:1, one launch (start us, length us, event | category | flops | bytes accessed | tf_op | source)
XLA Modules:
  0.0 105.0 jit_solution(986600723584783974)
XLA Ops:
  0.0 101.2 %one_round.1 = (s32[2,16,8,2,128]{4,3,2,1,0:T(2,128)S(1)}, f32[256,128]{1,0:T(8,128)S(1)}, s32[32,128]{1,0:T(8,128)S(1)}, s32[40,128]{1,0:T(8,128)S(1)}, f32[8,1...) custom-call(s32[8,128]{1,0:T(8,128)} %cand_hbm.1, ...), custom_call_target="tpu_custom_call" | custom-call | tf_op jit(solution)/shard_map/one_round/pallas_call | solution.py:508
  101.2 3.8 %merge.1 = f32[32,1024]{1,0:T(8,128)} custom-call(s32[2,128,2,128]{3,2,1,0:T(2,128)S(1)} %bitcast.4, f32[256,128]{1,0:T(8,128)S(1)} %get-tuple-element.15.near_ref, s32[1,4096]{1,0:T(1,128)S(1)} %bitcast.5, s32[40,128]{1,0:T(8,128)S(1)} %get-tuple-element.17.row_ref, f32[8,128]{1,0:T(8,128)S(1)} %get-tuple-element.18.info_ref, ...), custom_call_target="tpu_custom_call" | custom-call | tf_op jit(solution)/shard_map/merge/pallas_call | solution.py:672
